TPU v7x, 512 devices: a whole 4x4x16 slice. The times are simulated.
512 devices in a mesh: section: 8 (over y, x_hi), patch: 64 (over z, x_lo, core).
Axes of the slice: x: 4 (x_hi: 2, x_lo: 2; x = x_hi * 2 + x_lo), y: 4, z: 16, core: 2. Of those that a mesh axis runs over, the one named last changes fastest.
Arguments:
- states: bfloat16 [8, 128, 3072], P('section', 'patch'), may hold values from -6 to 6
- w_qkv: bfloat16 [8, 3072, 4608], P('section', None, 'patch'), may hold values from -0.109375 to 0.109375
- w_out: bfloat16 [8, 1536, 3072], P('section', None, 'patch'), may hold values from -0.15625 to 0.15625
- mod_table: float32 [28, 8, 3, 3072], P(None, 'section'), may hold values from -3 to 3
- q_gain: float32 [8, 128], P('section'), may hold values from 0.5 to 2.5
- k_gain: float32 [8, 128], P('section'), may hold values from 0.5 to 2.5
- stale_kv: bfloat16 [8, 8, 128, 3072], P('section', None, 'patch'), may hold values from -6 to 6
- timestep: int32 [8], replicated, may hold values from 0 to 27
- patch_order: int32 [64], replicated, may hold values from 0 to 63, each once
Outputs:
- next_states: bfloat16 [8, 128, 3072], P('section', 'patch')
Inputs may be any that keep to these rules, and one draw needn't show every extreme that they name: `patch_order`: every patch has one place, every place one patch.
All inputs are finite; a program needn't handle non-finite values.
Results may differ from a plain program's by a relative error of at most 0.015.
Values may be sent and summed in bfloat16 or wider, within the bound.
A program may use at most 64 MiB of HBM per device.

v0:
```python
import jax
import jax.numpy as jnp
from jax import lax
from jax.sharding import PartitionSpec as P

TICKS = 2


def passed_along(block, axis, distance):
    devices = range(lax.axis_size(axis))
    route = [((i - distance) % len(devices), i) for i in devices]
    return lax.ppermute(block, axis, route)


def modulate(state, row):
    values = state.astype(jnp.float32)
    center = values - jnp.mean(values, axis=-1, keepdims=True)
    spread = jnp.mean(center * center, axis=-1, keepdims=True)
    normed = center * lax.rsqrt(spread + 1e-06)
    return (normed * (1.0 + row[1]) + row[0]).astype(jnp.bfloat16)


def head_norm(values, gain):
    square = jnp.mean(values * values, axis=-1, keepdims=True)
    return values * lax.rsqrt(square + 1e-06) * gain


def rotate(values, positions):
    half = values.shape[-1] // 2
    freq = jnp.exp(-jnp.log(10000.0) * jnp.arange(half, dtype=jnp.float32) / half)
    angle = positions[:, None] * freq[None, :]
    cosine = jnp.cos(angle)[:, None, :]
    sine = jnp.sin(angle)[:, None, :]
    first = values[..., :half]
    second = values[..., half:]
    return jnp.concatenate(
        [first * cosine - second * sine, first * sine + second * cosine], axis=-1
    )


def fresh_part(query, key, value):
    dim = query.shape[2]
    scores = jnp.einsum(
        "qhd,khd->qhk", query.astype(jnp.float32), key.astype(jnp.float32)
    ) * dim ** (-0.5)
    top = jnp.max(scores, axis=-1)
    weights = jnp.exp(scores - top[..., None])
    total = jnp.sum(weights, axis=-1)
    summed = jnp.einsum("qhk,khd->qhd", weights, value.astype(jnp.float32))
    return (top, total, summed)


def fold_keys(carry, query, piece, own_low, own_count):
    top, total, summed = carry
    count = piece.shape[0]
    heads = query.shape[1]
    dim = query.shape[2]
    width = heads * dim
    keys = piece[:, :width].astype(jnp.float32).reshape(count, heads, dim)
    values = piece[:, width:].astype(jnp.float32).reshape(count, heads, dim)
    scores = jnp.einsum("qhd,khd->qhk", query.astype(jnp.float32), keys) * dim ** (-0.5)
    index = jnp.arange(count, dtype=jnp.int32)
    keep = (index < own_low) | (index >= own_low + own_count)
    scores = jnp.where(keep[None, None, :], scores, -1e30)
    new_top = jnp.maximum(top, jnp.max(scores, axis=-1))
    shrink = jnp.exp(top - new_top)
    weights = jnp.exp(scores - new_top[..., None])
    new_total = total * shrink + jnp.sum(weights, axis=-1)
    new_summed = summed * shrink[..., None] + jnp.einsum("qhk,khd->qhd", weights, values)
    return (new_top, new_total, new_summed)


def per_device(states, w_qkv, w_out, mod_table, q_gain, k_gain, stale_kv, timestep, patch_order):
    sections = lax.axis_size("section")
    section = lax.axis_index("section")
    patch = lax.axis_index("patch")
    count = states.shape[1]
    dim = q_gain.shape[1]
    width = w_out.shape[1]
    heads = width // dim
    images = [(section - tick) % sections for tick in range(TICKS)]
    mod_rows = [
        lax.dynamic_index_in_dim(
            mod_table, lax.dynamic_index_in_dim(timestep, image, 0, False), 0, False
        )[0]
        for image in images
    ]
    proj_in = w_qkv[0]
    proj_out = w_out[0]
    place = lax.dynamic_index_in_dim(patch_order, patch, 0, False)
    positions = (place * count + jnp.arange(count, dtype=jnp.int32)).astype(jnp.float32)
    own_low = patch * count
    caches = [lax.dynamic_index_in_dim(stale_kv[0], image, 0, False) for image in images]
    state = states[0]
    for tick in range(TICKS):
        row = mod_rows[tick]
        mixed = modulate(state, row)
        columns = jnp.dot(
            lax.all_gather(mixed, "patch", axis=0, tiled=True),
            proj_in,
            preferred_element_type=jnp.float32,
        ).astype(jnp.bfloat16)
        qkv = lax.all_to_all(columns, "patch", split_axis=0, concat_axis=1, tiled=True)
        query = qkv[:, :width].astype(jnp.float32).reshape(count, heads, dim)
        key = qkv[:, width : 2 * width].astype(jnp.float32).reshape(count, heads, dim)
        value = qkv[:, 2 * width :].reshape(count, heads, dim)
        query = rotate(head_norm(query, q_gain[0]), positions).astype(jnp.bfloat16)
        key = rotate(head_norm(key, k_gain[0]), positions).astype(jnp.bfloat16)
        initial = fresh_part(query, key, value)
        carry = fold_keys(
            initial,
            query,
            lax.all_gather(caches[tick], "patch", axis=0, tiled=True),
            own_low,
            count,
        )
        attended = (carry[2] / carry[1][..., None]).astype(jnp.bfloat16).reshape(count, width)
        out_columns = jnp.dot(
            lax.all_gather(attended, "patch", axis=0, tiled=True),
            proj_out,
            preferred_element_type=jnp.float32,
        )
        projected = lax.all_to_all(out_columns, "patch", split_axis=0, concat_axis=1, tiled=True)
        result = (state.astype(jnp.float32) + row[2] * projected).astype(jnp.bfloat16)
        state = passed_along(result[None], "section", 1)[0]
    return state[None]


def solution(mesh):
    in_specs = (
        P("section", "patch", None),
        P("section", None, "patch"),
        P("section", None, "patch"),
        P(None, "section", None, None),
        P("section", None),
        P("section", None),
        P("section", None, "patch", None),
        P(),
        P(),
    )
    out_specs = P("section", "patch", None)
    return jax.shard_map(
        per_device, mesh=mesh, in_specs=in_specs, out_specs=out_specs, check_vma=False
    )
```

profile of v0, /device:TPU:1, one launch (start us, length us, event | category | flops | bytes accessed | tf_op | source)
XLA Modules:
  0.0 496.4 jit_solution(14298856832202079918)
XLA Ops:
  0.0 1.4 fusion.64
  4.1 0.8 convert_reduce_fusion.1
  4.9 0.9 fusion.27
  7.2 0.8 constant_dynamic-slice_fusion
  8.0 0.8 fusion.49
  8.8 73.1 %all-gather.2 = bf16[64,2,3072]{2,1,0:T(2,128)(2,1)S(1)} all-gather(bf16[1,2,3072]{2,1,0:T(2,128)(2,1)S(1)} %fusion.49), channel_id=1, replica_groups=mesh['section'=8,'patch'=64] {'patch'}, dimensions={0}, use_global_device_ids=true | all-gather | bytes 798720 | tf_op jit(solution)/shard_map/all_gather | solution.py:99
  82.3 0.4 convolution_convert_fusion.1
  82.7 0.7 copy.28
  83.4 6.9 %all-to-all-start = ((bf16[64,2,72]{2,1,0:T(2,128)(2,1)}), bf16[64,2,72]{2,1,0:T(2,128)(2,1)S(1)}, u32[]{:S(2)}, u32[]{:S(2)}) async-start(bf16[64,2,72]{2,1,0:T(2,128)(2,1)} %bitcast.7), calls=%async_computation | async-start | bytes 65536 | tf_op jit(solution)/shard_map/all_to_all | solution.py:103
  90.3 0.7 constant_dynamic-slice_fusion.2
  91.1 67.9 %all-gather = bf16[1,1,128,3072]{3,1,0,2:T(2,128)(2,1)S(1)} all-gather(bf16[1,1,2,3072]{3,1,0,2:T(2,128)(2,1)S(1)} %copy.54), channel_id=2, replica_groups=mesh['section'=8,'patch'=64] {'patch'}, dimensions={2}, use_global_device_ids=true | all-gather | bytes 798720 | tf_op jit(solution)/shard_map/all_gather | solution.py:113
  159.0 1.8 copy.32
  160.8 0.6 dynamic_slice.27
  163.5 0.3 convolution_bitcast_fusion.3
  164.1 60.6 %all-gather.3 = bf16[64,2,1536]{2,1,0:T(2,128)(2,1)S(1)} all-gather(bf16[1,2,1536]{2,1,0:T(2,128)(2,1)S(1)} %fusion.13), channel_id=1, replica_groups=mesh['section'=8,'patch'=64] {'patch'}, dimensions={0}, use_global_device_ids=true | all-gather | bytes 399360 | tf_op jit(solution)/shard_map/all_gather | solution.py:119
  225.0 0.7 copy.36
  225.7 11.0 %all-to-all-start.1 = ((f32[64,2,48]{2,1,0:T(2,128)}), f32[64,2,48]{2,1,0:T(2,128)S(1)}, u32[]{:S(2)}, u32[]{:S(2)}) async-start(f32[64,2,48]{2,1,0:T(2,128)} %copy.36), calls=%async_computation.1 | async-start | bytes 131072 | tf_op jit(solution)/shard_map/all_to_all | solution.py:123
  236.8 14.4 %all-to-all-done.1 = f32[64,2,48]{2,1,0:T(2,128)S(1)} async-done(((f32[64,2,48]{2,1,0:T(2,128)}), f32[64,2,48]{2,1,0:T(2,128)S(1)}, u32[]{:S(2)}, u32[]{:S(2)}) %all-to-all-start.1) | async-done | bytes 24608 | tf_op jit(solution)/shard_map/all_to_all | solution.py:123
  251.3 4.6 collective-permute-start
  255.9 64.4 %all-gather.1 = bf16[1,1,128,3072]{3,1,0,2:T(2,128)(2,1)S(1)} all-gather(bf16[1,1,2,3072]{3,1,0,2:T(2,128)(2,1)S(1)} %copy.55), channel_id=3, replica_groups=mesh['section'=8,'patch'=64] {'patch'}, dimensions={2}, use_global_device_ids=true | all-gather | bytes 798720 | tf_op jit(solution)/shard_map/all_gather | solution.py:113
  320.4 1.8 copy.42
  322.6 63.3 %all-gather.4 = bf16[64,2,3072]{2,1,0:T(2,128)(2,1)S(1)} all-gather(bf16[1,2,3072]{2,1,0:T(2,128)(2,1)S(1)} %fusion.48), channel_id=1, replica_groups=mesh['section'=8,'patch'=64] {'patch'}, dimensions={0}, use_global_device_ids=true | all-gather | bytes 798720 | tf_op jit(solution)/shard_map/all_gather | solution.py:99
  386.2 0.4 convolution_convert_fusion
  386.6 0.7 copy.38
  387.3 4.4 all-to-all-start.2
  391.8 13.1 %all-to-all-done.2 = bf16[64,2,72]{2,1,0:T(2,128)(2,1)S(1)} async-done(((bf16[64,2,72]{2,1,0:T(2,128)(2,1)}), bf16[64,2,72]{2,1,0:T(2,128)(2,1)S(1)}, u32[]{:S(2)}, u32[]{:S(2)}) %all-to-all-start.2) | async-done | bytes 18464 | tf_op jit(solution)/shard_map/all_to_all | solution.py:103
  406.2 0.3 convolution_bitcast_fusion.2
  406.8 61.4 %all-gather.5 = bf16[64,2,1536]{2,1,0:T(2,128)(2,1)S(1)} all-gather(bf16[1,2,1536]{2,1,0:T(2,128)(2,1)S(1)} %fusion.15), channel_id=1, replica_groups=mesh['section'=8,'patch'=64] {'patch'}, dimensions={0}, use_global_device_ids=true | all-gather | bytes 399360 | tf_op jit(solution)/shard_map/all_gather | solution.py:119
  468.6 19.0 %all_to_all.70 = f32[64,2,48]{2,1,0:T(2,128)S(1)} all-to-all(f32[64,2,48]{2,1,0:T(2,128)S(1)} %copy.46), channel_id=1, replica_groups=mesh['section'=8,'patch'=64] {'patch'}, dimensions={0} | all-to-all | bytes 49152 | tf_op jit(solution)/shard_map/all_to_all | solution.py:123
  487.7 4.3 collective-permute-start.1
  492.0 3.8 collective-permute-done.1
  495.8 0.6 copy.61
  (67 shorter events, 5.2 us)
Async XLA Ops:
  0.0 82.3 %copy-start = (bf16[1,3072,72]{1,2,0:T(8,128)(2,1)S(1)}, bf16[1,3072,72]{1,2,0:T(8,128)(2,1)}, u32[]{:S(2)}) copy-start(bf16[1,3072,72]{1,2,0:T(8,128)(2,1)} %param.10) | copy-start | bytes 1327108
  83.4 78.8 %all-to-all-start = ((bf16[64,2,72]{2,1,0:T(2,128)(2,1)}), bf16[64,2,72]{2,1,0:T(2,128)(2,1)S(1)}, u32[]{:S(2)}, u32[]{:S(2)}) async-start(bf16[64,2,72]{2,1,0:T(2,128)(2,1)} %bitcast.7), calls=%async_computation | async-start | bytes 65536 | tf_op jit(solution)/shard_map/all_to_all | solution.py:103
  159.0 1.8 copy-start.5
  159.0 3.5 copy-start.2
  159.0 3.5 copy-start.3
  160.7 64.0 %copy-start.4 = (bf16[1,1536,48]{1,2,0:T(8,128)(2,1)S(1)}, bf16[1,1536,48]{1,2,0:T(8,128)(2,1)}, u32[]{:S(2)}) copy-start(bf16[1,1536,48]{1,2,0:T(8,128)(2,1)} %param.11) | copy-start | bytes 442372
  162.6 88.7 %copy-start.1 = (bf16[1,2,3072]{2,1,0:T(2,128)(2,1)S(1)}, bf16[1,2,3072]{2,1,0:T(2,128)(2,1)}, u32[]{:S(2)}) copy-start(bf16[1,2,3072]{2,1,0:T(2,128)(2,1)} %param.9) | copy-start | bytes 36868
  225.7 25.4 %all-to-all-start.1 = ((f32[64,2,48]{2,1,0:T(2,128)}), f32[64,2,48]{2,1,0:T(2,128)S(1)}, u32[]{:S(2)}, u32[]{:S(2)}) async-start(f32[64,2,48]{2,1,0:T(2,128)} %copy.36), calls=%async_computation.1 | async-start | bytes 131072 | tf_op jit(solution)/shard_map/all_to_all | solution.py:123
  251.3 70.8 %collective-permute-start = (bf16[1,2,3072]{2,1,0:T(2,128)(2,1)S(1)}, bf16[1,2,3072]{2,1,0:T(2,128)(2,1)S(1)}, u32[]{:S(2)}, u32[]{:S(2)}) collective-permute-start(bf16[1,2,3072]{2,1,0:T(2,128)(2,1)S(1)} %fusion.31), channel_id=1, source_target_pairs={{448,0},{0,64},{64,128},{128,192},{192,256},{256,320},{320,384},{3... | collective-permute-start | bytes 36872 | tf_op jit(solution)/shard_map/ppermute | solution.py:12
  387.3 17.6 %all-to-all-start.2 = ((bf16[64,2,72]{2,1,0:T(2,128)(2,1)}), bf16[64,2,72]{2,1,0:T(2,128)(2,1)S(1)}, u32[]{:S(2)}, u32[]{:S(2)}) async-start(bf16[64,2,72]{2,1,0:T(2,128)(2,1)} %bitcast.34), calls=%async_computation.2 | async-start | bytes 65536 | tf_op jit(solution)/shard_map/all_to_all | solution.py:103
  487.7 8.1 %collective-permute-start.1 = (bf16[1,2,3072]{2,1,0:T(2,128)(2,1)S(1)}, bf16[1,2,3072]{2,1,0:T(2,128)(2,1)S(1)}, u32[]{:S(2)}, u32[]{:S(2)}) collective-permute-start(bf16[1,2,3072]{2,1,0:T(2,128)(2,1)S(1)} %fusion.39), channel_id=1, source_target_pairs={{448,0},{0,64},{64,128},{128,192},{192,256},{256,320},{320,384},{3... | collective-permute-start | bytes 36872 | tf_op jit(solution)/shard_map/ppermute | solution.py:12
where the time goes:
time: 497 us; the launch traced here: 496 us
  blocking collectives  410 us (82%)
  waiting for transfers between devices  31.3 us (6%)
  starting transfers between devices  31.2 us (6%)
  local copies, waits for them, and re-layouts  10.3 us (2%)
  between operations  5.11 us (1%)
  other arithmetic  5.09 us (1%)
    all_gather x2, blocking collectives, per_device(): lax.all_gather(mixed, 'patch', axis=0, tiled=True)  136 us
    all_gather x2, blocking collectives, per_device(): lax.all_gather(caches[tick], 'patch', axis=0, tiled=True)  132 us
    all_gather x2, blocking collectives, per_device(): lax.all_gather(attended, 'patch', axis=0, tiled=True)  122 us
    all_to_all x1, blocking collectives, per_device(): lax.all_to_all(out_columns, 'patch', split_axis=0, concat_axis=1, tiled=T...  19 us
    all_to_all x1, waiting for transfers between devices, per_device(): lax.all_to_all(out_columns, 'patch', split_axis=0, concat_axis=1, tiled=T...  14.4 us
    all_to_all x2, waiting for transfers between devices, per_device(): lax.all_to_all(columns, 'patch', split_axis=0, concat_axis=1, tiled=True)  13.1 us
    all_to_all x2, starting transfers between devices, per_device(): lax.all_to_all(columns, 'patch', split_axis=0, concat_axis=1, tiled=True)  11.4 us
    all_to_all x1, starting transfers between devices, per_device(): lax.all_to_all(out_columns, 'patch', split_axis=0, concat_axis=1, tiled=T...  11 us
  transfers between devices with their start and end apart: 5, of which 3 were waited for; matrix products, arithmetic and copies ran while one was open for 1% of the time, Pallas kernels for 0%

commit v1 on v0

v1 whole, which is shorter than its diff:
```python
import functools

import jax
import jax.numpy as jnp
from jax import lax
from jax.experimental import pallas as pl
from jax.experimental.pallas import tpu as pltpu
from jax.sharding import PartitionSpec as P

MESH = pl.DeviceIdType.MESH
F32 = jnp.float32
BF16 = jnp.bfloat16
NZ = 16
NS = 8
BLK = 48
HEADS = 12
D = 3072
KC = D // 128
QROWS = 72
LAG = 4


def owner_of(head):
    part = (head % 3) * HEADS + head
    centre = (128 * part + 64) // QROWS
    return (centre // 4) * 4 + head % 4


def dot_nt(a, b):
    return lax.dot_general(a, b, (((1,), (1,)), ((), ())), preferred_element_type=F32)


def dot_nn(a, b):
    return lax.dot_general(a, b, (((1,), (0,)), ((), ())), preferred_element_type=F32)


def kernel(
    x_hbm, wq_hbm, wo_hbm, mod_hbm, st_hbm, order_ref, qg_ref, kg_ref, time_ref,
    out_ref,
    x_in, wq, wo, mod, st_in, rows_f, st_src, gran_f,
    g0, g1, wide, xr, wmod, pick, colv, table, gains,
    qsrc, qrecv, stale, stale_f, keys, vals, att, ysrc, dsrc, drecv,
    load_sem, ready, nready,
    ag_send, ag_own, ag_x, ag_core, ag_diag,
    st_send, st_recv, q_send, q_recv,
    at_send, at_own, at_x, at_core, at_diag,
    d_send, d_recv,
):
    s = lax.axis_index("section")
    p = lax.axis_index("patch")
    z = p // 4
    cls = p % 4
    xl = cls // 2
    core = p % 2
    after = (s + 1) % NS
    before = (s + NS - 1) % NS
    zbase = z * 4
    core_mate = zbase + xl * 2 + (1 - core)
    x_mate = zbase + (1 - xl) * 2 + core
    diag_mate = zbase + (1 - xl) * 2 + (1 - core)

    loads = [
        pltpu.make_async_copy(x_hbm, x_in, load_sem.at[0]),
        pltpu.make_async_copy(st_hbm.at[s], st_in.at[0], load_sem.at[1]),
        pltpu.make_async_copy(st_hbm.at[before], st_in.at[1], load_sem.at[2]),
        pltpu.make_async_copy(wq_hbm, wq, load_sem.at[3]),
        pltpu.make_async_copy(mod_hbm, mod, load_sem.at[4]),
        pltpu.make_async_copy(wo_hbm, wo, load_sem.at[5]),
    ]
    for load in loads:
        load.start()

    barrier = pltpu.get_barrier_semaphore()

    def greet(sec, dev):
        pl.semaphore_signal(barrier, inc=1, device_id=(sec, dev), device_id_type=MESH)

    def greet_line(i, _):
        greet(s, ((z + i) % NZ) * 4 + cls)
        return 0

    lax.fori_loop(1, NZ, greet_line, 0)
    for mate in (core_mate, x_mate, diag_mate):
        greet(s, mate)
    greet(after, p)
    greet(before, p)

    loads[0].wait()
    xf = x_in[...].astype(F32)
    for t in range(2):
        for k in range(KC):
            rows_f[pl.ds(t * KC + k, 1), :] = xf[t : t + 1, k * 128 : (k + 1) * 128]
    own = pl.ds(pl.multiple_of(p * BLK, 16), BLK)
    g0[own, :] = rows_f[...].astype(BF16)
    loads[1].wait()
    loads[2].wait()
    for tick in range(2):
        sf = st_in[tick].astype(F32)
        for kv in range(2):
            for head in range(HEADS):
                for t in range(2):
                    row = (head // 2) * 16 + (((head % 2) * 2 + tick) * 2 + kv) * 2 + t
                    low = (kv * HEADS + head) * 128
                    gran_f[pl.ds(row, 1), :] = sf[t : t + 1, low : low + 128]
    st_src[...] = gran_f[...].astype(BF16)

    pl.semaphore_wait(barrier, 20)

    def block(g, b):
        return g.at[pl.ds(pl.multiple_of(b * BLK, 16), BLK)]

    def push(src, dst, send, recv, sec, dev):
        pltpu.make_async_remote_copy(
            src_ref=src, dst_ref=dst, send_sem=send, recv_sem=recv,
            device_id=(sec, dev), device_id_type=MESH,
        ).start()

    def take(ref, sem):
        pltpu.make_async_copy(ref, ref, sem).wait()

    def line_z(i):
        far = (i + 1) // 2
        return (z + NZ + far * (2 * (i % 2) - 1)) % NZ

    def relay_own(g, tick, zs):
        b = zs * 4 + cls
        push(block(g, b), block(g, b), ag_send.at[tick], ag_core.at[tick], s, core_mate)
        push(block(g, b), block(g, b), ag_send.at[tick], ag_x.at[tick, zs], s, x_mate)

    def relay_x(g, tick, zs):
        b = zs * 4 + (1 - xl) * 2 + core
        take(block(g, b), ag_x.at[tick, zs])
        push(block(g, b), block(g, b), ag_send.at[tick], ag_diag.at[tick], s, core_mate)

    def relay_steps(g, tick, first, last):
        def step(i, _):
            zs = line_z(i)
            take(block(g, zs * 4 + cls), ag_own.at[tick, zs])
            relay_own(g, tick, zs)

            @pl.when(i >= LAG)
            def _():
                relay_x(g, tick, line_z(i - LAG))

            return 0

        lax.fori_loop(first, last, step, 0)

    def relay_tail(g, tick):
        def step(i, _):
            relay_x(g, tick, line_z(i))
            return 0

        lax.fori_loop(NZ - LAG, NZ, step, 0)
        some = g.at[pl.ds(0, NZ * BLK)]
        take(some, ag_core.at[tick])
        take(some, ag_diag.at[tick])

    def first_send(i, _):
        dev = line_z(NZ - i) * 4 + cls
        push(g0.at[own], g0.at[own], ag_send.at[0], ag_own.at[0, z], s, dev)
        return 0

    lax.fori_loop(1, NZ, first_send, 0)
    for mate in (core_mate, x_mate, diag_mate):
        pl.semaphore_signal(ready, inc=1, device_id=(s, mate), device_id_type=MESH)
    relay_own(g0, 0, z)
    pl.semaphore_wait(ready, 3)
    pl.semaphore_signal(nready, inc=1, device_id=(before, p), device_id_type=MESH)

    for head in range(HEADS):
        dev = owner_of(head)
        src = st_src.at[pl.ds((head // 2) * 16, 16)]
        dst = stale.at[pl.ds(pl.multiple_of(p * 16, 16), 16)]

        @pl.when(p == dev)
        def _():
            pltpu.make_async_copy(src, dst, st_recv).start()

        @pl.when(p != dev)
        def _():
            push(src, dst, st_send, st_recv, s, dev)

    my_head = jnp.int32(0)
    owned = jnp.int32(0)
    for head in range(HEADS):
        hit = jnp.where(p == owner_of(head), 1, 0)
        my_head = my_head + head * hit
        owned = owned + hit

    for load in loads[3:]:
        load.wait()
    times = [time_ref[s], time_ref[before]]
    feature = lax.broadcasted_iota(jnp.int32, (BLK, 128), 1)
    mine = p * BLK + lax.broadcasted_iota(jnp.int32, (BLK, 128), 0)
    for k in range(KC):
        lanes = pl.ds(k * 128, 128)
        pick[:, lanes] = jnp.where(feature + k * 128 == mine, 1.0, 0.0).astype(BF16)
    for tick in range(2):
        shift_sum = jnp.zeros((QROWS, 128), F32)
        row_sum = jnp.zeros((QROWS, 128), F32)
        gate_sum = jnp.zeros((BLK, 128), F32)
        base = times[tick] * 3
        for k in range(KC):
            lanes = pl.ds(k * 128, 128)
            shift = mod[base, :, lanes]
            scale = mod[base + 1, :, lanes]
            gate = mod[base + 2, :, lanes]
            w = wq[:, lanes].astype(F32)
            scaled = (w * (1.0 + scale)).astype(BF16)
            wmod[tick, :, lanes] = scaled
            shift_sum += w * shift
            row_sum += scaled.astype(F32)
            gate_sum += jnp.where(pick[:, lanes].astype(F32) > 0.5, gate, 0.0)
        for j, value in enumerate((shift_sum, row_sum)):
            total = jnp.sum(value, axis=1, keepdims=True)
            colv[tick, j, pl.ds(0, QROWS), :] = jnp.broadcast_to(total, (QROWS, 128))
        total = jnp.sum(gate_sum, axis=1, keepdims=True)
        colv[tick, 2, pl.ds(0, BLK), :] = jnp.broadcast_to(total, (BLK, 128))

    @pl.when(owned == 1)
    def _():
        r = lax.broadcasted_iota(jnp.int32, (128, 128), 0)
        c = lax.broadcasted_iota(jnp.int32, (128, 128), 1)
        for j, ref in enumerate((qg_ref, kg_ref)):
            diag = jnp.where(r == c, jnp.broadcast_to(ref[...], (128, 128)), 0.0)
            gains[j] = jnp.broadcast_to(jnp.sum(diag, axis=1, keepdims=True), (128, 128))
        pr = lax.broadcasted_iota(jnp.int32, (64, 128), 0)
        pc = lax.broadcasted_iota(jnp.int32, (64, 128), 1)
        low = jnp.where(pc < 64, pc, pc - 64)
        column = order_ref[...].astype(F32)
        place = jnp.sum(jnp.where(pr == low, column, 0.0), axis=0, keepdims=True)
        pos = place * 2.0 + jnp.where(pc[:1] < 64, 0.0, 1.0)
        freq = jnp.exp(pr.astype(F32) * (-jnp.log(F32(10000.0)) / 64.0))
        angle = pos * freq
        table[0] = jnp.cos(angle)
        table[1] = jnp.sin(angle)

    relay_steps(g0, 0, 1, NZ)
    relay_tail(g0, 0)

    def send_qkv(tick):
        for i in range(9):
            unit = p * 9 + i
            part = unit // 16
            head = part % HEADS
            dev = owner_of(head)
            kind = part // HEADS
            row = pl.multiple_of(kind * 128 + (unit % 16) * 8, 8)
            src = qsrc.at[tick, pl.ds(i * 8, 8)]
            dst = qrecv.at[tick, pl.ds(row, 8)]

            @pl.when(p == dev)
            def _():
                pltpu.make_async_copy(src, dst, q_recv.at[tick]).start()

            @pl.when(p != dev)
            def _():
                push(src, dst, q_send.at[tick], q_recv.at[tick], s, dev)

    def finish_qkv(tick, acc, mean, var):
        rstd = lax.rsqrt(var + 1e-06)
        shift = colv[tick, 0, pl.ds(0, QROWS), :]
        rows = colv[tick, 1, pl.ds(0, QROWS), :]
        qkv = rstd * (acc - rows * mean) + shift
        qsrc[tick] = qkv.astype(BF16).astype(F32)

    for b in range(24):
        part = pl.ds(b * 128, 128)
        wide[part, :] = g0[part, :].astype(F32)
    total = jnp.zeros((128, 128), F32)
    for k in range(KC):
        piece = jnp.concatenate(
            [wide[pl.ds(k, 64, stride=BLK), :], wide[pl.ds(KC + k, 64, stride=BLK), :]],
            axis=0,
        )
        total += piece
        xr[:, pl.ds(k * 128, 128)] = piece.astype(BF16)
    acc0 = dot_nt(wmod[0], xr[...])
    mean_c = jnp.sum(total, axis=1, keepdims=True) * (1.0 / D)
    total = jnp.zeros((128, 128), F32)
    for k in range(KC):
        centred = xr[:, pl.ds(k * 128, 128)].astype(F32) - mean_c
        total += centred * centred
    var_c = jnp.sum(total, axis=1, keepdims=True) * (1.0 / D)
    lane = lax.broadcasted_iota(jnp.int32, (128, 128), 1)
    stats = jnp.transpose(jnp.where(lane < 64, mean_c, var_c))
    finish_qkv(0, acc0, stats[0:1, :], stats[64:65, :])
    send_qkv(0)
    x_own = dot_nt(pick[...], xr[...])

    @pl.when(owned == 1)
    def _():
        take(stale, st_recv)
        for b in range(8):
            part = pl.ds(b * 128, 128)
            stale_f[part, :] = stale[part, :].astype(F32)
        second = my_head % 2
        for tick in range(2):
            got = []
            for kv in range(2):
                both = [
                    stale_f[pl.ds(second * 8 + (tick * 2 + kv) * 2 + t, 64, stride=16), :]
                    for t in range(2)
                ]
                got.append(jnp.concatenate(both, axis=0))
            keys[tick] = got[0].astype(BF16)
            vals[tick] = jnp.transpose(got[1]).astype(BF16)

    def attend(tick):
        take(qrecv.at[tick], q_recv.at[tick])
        factor = 128.0 ** -0.5
        cosine, sine = table[0], table[1]

        def prepared(low, j):
            u = qrecv[tick, pl.ds(low, 128), :]
            square = jnp.sum(u * u, axis=0, keepdims=True) * (1.0 / 128)
            u = u * lax.rsqrt(square + 1e-06) * gains[j]
            a, b = u[:64], u[64:]
            return jnp.concatenate(
                [a * cosine - b * sine, a * sine + b * cosine], axis=0
            ).astype(BF16)

        query = prepared(0, 0)
        key = prepared(128, 1).astype(F32)
        value = qrecv[tick, pl.ds(256, 128), :]
        scores = dot_nn(keys[tick], query) * factor
        r = lax.broadcasted_iota(jnp.int32, (128, 128), 0)
        c = lax.broadcasted_iota(jnp.int32, (128, 128), 1)
        away = jnp.abs(r - c)
        scores = jnp.where((away == 0) | (away == 64), -1e30, scores)
        wide_q = query.astype(F32)
        same = jnp.sum(wide_q * key, axis=0, keepdims=True) * factor
        other = jnp.sum(wide_q * pltpu.roll(key, 64, 1), axis=0, keepdims=True) * factor
        top = jnp.maximum(jnp.max(scores, axis=0, keepdims=True), jnp.maximum(same, other))
        weights = jnp.exp(scores - top)
        same = jnp.exp(same - top)
        other = jnp.exp(other - top)
        mass = jnp.sum(weights, axis=0, keepdims=True) + same + other
        summed = dot_nn(vals[tick], weights.astype(BF16))
        summed = summed + same * value + other * pltpu.roll(value, 64, 1)
        rows = pl.ds(pl.multiple_of(my_head * 128, 128), 128)
        att[tick, rows, :] = (summed / mass).astype(BF16)

        def send(i, _):
            dev = line_z(NZ - i) * 4 + cls
            piece = att.at[tick, rows]
            push(piece, piece, at_send.at[tick], at_own.at[tick, my_head // 4], s, dev)
            return 0

        lax.fori_loop(1, NZ, send, 0)

    def head_rows(tick, head):
        return att.at[tick, pl.ds(pl.multiple_of(head * 128, 128), 128)]

    def gather_attended(tick):
        for j in range(3):
            head = j * 4 + cls
            piece = head_rows(tick, head)

            @pl.when(owner_of(head) != p)
            def _():
                take(piece, at_own.at[tick, j])

            push(piece, piece, at_send.at[tick], at_core.at[tick], s, core_mate)
            push(piece, piece, at_send.at[tick], at_x.at[tick, j], s, x_mate)
        for j in range(3):
            head = j * 4 + (1 - xl) * 2 + core
            piece = head_rows(tick, head)
            take(piece, at_x.at[tick, j])
            push(piece, piece, at_send.at[tick], at_diag.at[tick], s, core_mate)
        some = att.at[tick, pl.ds(0, 3 * 128)]
        take(some, at_core.at[tick])
        take(some, at_diag.at[tick])

    def project(tick, residual):
        out = dot_nn(wo[...], att[tick])
        gate = colv[tick, 2, pl.ds(0, BLK), :]
        return (residual + gate * out).astype(BF16)

    @pl.when(owned == 1)
    def _():
        attend(0)

    gather_attended(0)
    ysrc[...] = project(0, x_own)

    pl.semaphore_wait(nready, 1)

    def second_send(i, _):
        dev = line_z(NZ - i) * 4 + cls
        push(ysrc, g1.at[own], ag_send.at[1], ag_own.at[1, z], after, dev)
        return 0

    lax.fori_loop(1, NZ + 1, second_send, 0)

    relay_steps(g1, 1, 0, NZ)
    relay_tail(g1, 1)
    acc1 = dot_nn(wmod[1], g1[...])
    total = jnp.zeros((128, 128), F32)
    for k in range(KC):
        total += g1[pl.ds(k * 128, 128), :].astype(F32)
    mean = jnp.sum(total, axis=0, keepdims=True) * (1.0 / D)
    total = jnp.zeros((128, 128), F32)
    for k in range(KC):
        centred = g1[pl.ds(k * 128, 128), :].astype(F32) - mean
        total += centred * centred
    var = jnp.sum(total, axis=0, keepdims=True) * (1.0 / D)
    finish_qkv(1, acc1, mean, var)
    send_qkv(1)

    @pl.when(owned == 1)
    def _():
        attend(1)

    gather_attended(1)
    last = project(1, g1[own, :].astype(F32)).astype(F32)
    stacked = jnp.concatenate(
        [last, pltpu.roll(last, 64, 1), jnp.zeros((32, 128), F32)], axis=0
    )
    turned = jnp.transpose(stacked)
    for i in range(64):
        dsrc[i] = turned[i : i + 1, :]

    def last_send(i, _):
        dev = (p + i) % 64
        push(dsrc.at[dev], drecv.at[p], d_send, d_recv, after, dev)
        return 0

    lax.fori_loop(0, 64, last_send, 0)
    take(drecv, d_recv)
    out_ref[...] = drecv[...]

    take(g0.at[pl.ds(0, 63 * BLK)], ag_send.at[0])
    take(g1, ag_send.at[1])
    take(dsrc, d_send)
    is_owner = owned == 1
    mine_units = jnp.int32(0)
    for i in range(9):
        mine_units = mine_units + jnp.where(
            owner_of(((p * 9 + i) // 16) % HEADS) == p, 1, 0
        )
    for tick in range(2):
        def drain(i, _):
            take(qsrc.at[tick, pl.ds(0, 8)], q_send.at[tick])
            return 0

        lax.fori_loop(0, 9 - mine_units, drain, 0)
        take(att.at[tick, pl.ds(0, 9 * 128)], at_send.at[tick])

        @pl.when(is_owner)
        def _():
            def drain_piece(i, _):
                take(att.at[tick, pl.ds(0, 128)], at_send.at[tick])
                return 0

            lax.fori_loop(1, NZ, drain_piece, 0)

    def drain_stale(i, _):
        take(st_src.at[pl.ds(0, 16)], st_send)
        return 0

    lax.fori_loop(0, HEADS - owned, drain_stale, 0)


def per_device(states, w_qkv, w_out, mod_table, q_gain, k_gain, stale_kv, timestep, patch_order):
    hbm = pl.BlockSpec(memory_space=pl.ANY)
    vmem = pl.BlockSpec(memory_space=pltpu.VMEM)
    dma = pltpu.SemaphoreType.DMA
    regular = pltpu.SemaphoreType.REGULAR
    got = pl.pallas_call(
        kernel,
        out_shape=jax.ShapeDtypeStruct((64, 1, 128), F32),
        in_specs=[hbm] * 5 + [vmem] * 3 + [pl.BlockSpec(memory_space=pltpu.SMEM)],
        out_specs=vmem,
        scratch_shapes=[
            pltpu.VMEM((2, D), BF16),
            pltpu.VMEM((QROWS, D), BF16),
            pltpu.VMEM((BLK, D // 2), BF16),
            pltpu.VMEM((84, 1, D), F32),
            pltpu.VMEM((2, 2, D), BF16),
            pltpu.VMEM((BLK, 128), F32),
            pltpu.VMEM((96, 128), BF16),
            pltpu.VMEM((96, 128), F32),
            pltpu.VMEM((D, 128), BF16),
            pltpu.VMEM((D, 128), BF16),
            pltpu.VMEM((D, 128), F32),
            pltpu.VMEM((128, D), BF16),
            pltpu.VMEM((2, QROWS, D), BF16),
            pltpu.VMEM((BLK, D), BF16),
            pltpu.VMEM((2, 3, QROWS, 128), F32),
            pltpu.VMEM((2, 64, 128), F32),
            pltpu.VMEM((2, 128, 128), F32),
            pltpu.VMEM((2, QROWS, 128), F32),
            pltpu.VMEM((2, 384, 128), F32),
            pltpu.VMEM((1024, 128), BF16),
            pltpu.VMEM((1024, 128), F32),
            pltpu.VMEM((2, 128, 128), BF16),
            pltpu.VMEM((2, 128, 128), BF16),
            pltpu.VMEM((2, D // 2, 128), BF16),
            pltpu.VMEM((BLK, 128), BF16),
            pltpu.VMEM((64, 1, 128), F32),
            pltpu.VMEM((64, 1, 128), F32),
            dma((6,)),
            regular,
            regular,
            dma((2,)),
            dma((2, NZ)),
            dma((2, NZ)),
            dma((2,)),
            dma((2,)),
            dma,
            dma,
            dma((2,)),
            dma((2,)),
            dma((2,)),
            dma((2, 3)),
            dma((2, 3)),
            dma((2,)),
            dma((2,)),
            dma,
            dma,
        ],
        compiler_params=pltpu.CompilerParams(
            collective_id=0, has_side_effects=True, vmem_limit_bytes=40 * 2**20
        ),
        name="block_cycle",
    )(
        states[0],
        w_qkv[0].T,
        w_out[0].T,
        jnp.transpose(mod_table, (0, 2, 1, 3)).reshape(84, 1, D),
        stale_kv[0],
        patch_order.reshape(64, 1),
        q_gain,
        k_gain,
        timestep,
    )
    pairs = got[:, 0, : 2 * BLK].reshape(64, 2, BLK)
    return jnp.transpose(pairs, (1, 0, 2)).reshape(1, 2, D).astype(BF16)


def solution(mesh):
    in_specs = (
        P("section", "patch", None),
        P("section", None, "patch"),
        P("section", None, "patch"),
        P(None, "section", None, None),
        P("section", None),
        P("section", None),
        P("section", None, "patch", None),
        P(),
        P(),
    )
    out_specs = P("section", "patch", None)
    return jax.shard_map(
        per_device, mesh=mesh, in_specs=in_specs, out_specs=out_specs, check_vma=False
    )
```

time: 497 us -> 121 us (0.24)
  blocking collectives: 410 us -> 0 us
  Pallas kernels: 0 us -> 114 us
  waiting for transfers between devices: 31.3 us -> 0 us
  starting transfers between devices: 31.2 us -> 0 us
  other arithmetic: 5.09 us -> 0 us
  between operations: 5.11 us -> 0.04 us
    all_gather x6 -> x0, blocking collectives: 391 us -> none  [the longest x2 136 us: per_device(): lax.all_gather(mixed, 'patch', axis=0, tiled=True)]
    pallas_call x0 -> x1, Pallas kernels: none -> 114 us  [per_device(): pl.pallas_call(kernel, out_shape=jax.ShapeDtypeStruct((64, 1, 128), F32),...]
    all_to_all x3 -> x0, waiting for transfers between devices: 27.5 us -> none  [the longest x1 14.4 us: per_device(): lax.all_to_all(out_columns, 'patch', split_axis=0, concat_axis=1, tiled=T...]
    all_to_all x3 -> x0, starting transfers between devices: 22.4 us -> none  [the longest x2 11.4 us: per_device(): lax.all_to_all(columns, 'patch', split_axis=0, concat_axis=1, tiled=True)]
    all_to_all x1 -> x0, blocking collectives: 19 us -> none  [per_device(): lax.all_to_all(out_columns, 'patch', split_axis=0, concat_axis=1, tiled=T...]
    ppermute x2 -> x0, starting transfers between devices: 8.88 us -> none  [passed_along(): return lax.ppermute(block, axis, route)]
  transfers between devices with their start and end apart: 5 -> 0, of which waited for: 3 -> 0; matrix products, arithmetic and copies ran while one was open for 1% -> 0% of each run, Pallas kernels for 0% -> 0%
where the time goes in v1:
time: 121 us
  Pallas kernels  114 us (94%)
  local copies, waits for them, and re-layouts  6.35 us (5%)
    pallas_call x1, Pallas kernels, per_device(): pl.pallas_call(kernel, out_shape=jax.ShapeDtypeStruct((64, 1, 128), F32),...  114 us
    unnamed x18, local copies, waits for them, and re-layouts  5.3 us

profile of v1, /device:TPU:1, one launch (start us, length us, event | category | flops | bytes accessed | tf_op | source)
XLA Modules:
  0.0 120.6 jit_solution(11534221348011157488)
XLA Ops:
  0.0 0.0 copy-start.8
  0.0 0.7 copy-done.8
  0.7 0.0 copy-start.4
  0.7 0.0 copy-start.5
  0.7 0.0 copy-start.6
  0.7 0.0 copy-start.7
  0.7 0.1 copy.12.order_ref
  0.8 0.6 copy-done.4
  1.4 0.0 copy-done.5
  1.4 0.0 copy-done.6
  1.4 0.0 copy-done.7
  1.4 0.0 copy-start
  1.4 1.2 %copy-done = f32[28,1,3,3072]{3,1,2,0:T(1,128)S(1)} copy-done((f32[28,1,3,3072]{3,1,2,0:T(1,128)S(1)}, f32[28,1,3,3072]{3,1,2,0:T(1,128)}, u32[]{:S(2)}) %copy-start) | copy-done | bytes 1032216
  2.6 0.0 copy-start.1
  2.6 1.0 copy-done.1
  3.6 0.0 copy-start.2
  3.6 0.9 copy-done.2
  4.5 0.0 copy-start.3
  4.5 0.9 copy-done.3
  5.4 114.2 %block_cycle.1 = f32[64,1,128]{2,1,0:T(1,128)S(1)} custom-call(bf16[2,3072]{1,0:T(2,128)(2,1)S(1)} %bitcast.17, bf16[72,3072]{1,0:T(8,128)(2,1)S(1)} %bitcast.14, bf16[48,1536]{1,0:T(8,128)(2,1)S(1)} %bitcast.15, f32[84,1,3072]{2,1,0:T(1,128)S(1)} %bitcast.13, bf16[8,2,3072]{2,1,0:T(2,128)(2,1)S(1)} %bitcast.16, s32[64,1]{1,0:T(8,128)S(1)} %copy.12.order_ref, ...), custom_call_target="tpu_custom_call" | custom-call | tf_op jit(solution)/shard_map/block_cycle/pallas_call | solution.py:471
  119.6 0.1 copy.13
  119.8 0.1 copy.14
  119.9 0.7 convert_element_type.20
  (1 shorter events, 0.0 us)
Async XLA Ops:
  0.0 0.7 copy-start.8
  0.7 0.7 copy-start.4
  0.7 0.7 copy-start.5
  0.7 0.7 copy-start.6
  0.7 0.7 copy-start.7
  1.4 1.2 %copy-start = (f32[28,1,3,3072]{3,1,2,0:T(1,128)S(1)}, f32[28,1,3,3072]{3,1,2,0:T(1,128)}, u32[]{:S(2)}) copy-start(f32[28,1,3,3072]{3,1,2,0:T(1,128)} %param.12) | copy-start | bytes 3096580
  2.6 1.0 copy-start.1
  3.6 0.9 copy-start.2
  4.5 0.9 copy-start.3

commit v2 on v1

v2 whole, which is shorter than its diff:
```python
import jax
import jax.numpy as jnp
from jax import lax
from jax.experimental import pallas as pl
from jax.experimental.pallas import tpu as pltpu
from jax.sharding import PartitionSpec as P

MESH = pl.DeviceIdType.MESH
F32 = jnp.float32
BF16 = jnp.bfloat16
NZ = 16
NS = 8
BLK = 48
HEADS = 12
PAIRS = 6
D = 3072
KC = D // 128
LINE = 32
QROWS = 72
REACH = 4
CHUNK = 768


def owner_of(pair, line):
    part = ((pair + line) % 3) * PAIRS + pair
    centre = (32 * part + 16) // 9
    return (centre // 4) * 4 + 2 * line + pair % 2


def dot_nt(a, b):
    return lax.dot_general(a, b, (((1,), (1,)), ((), ())), preferred_element_type=F32)


def dot_nn(a, b):
    return lax.dot_general(a, b, (((1,), (0,)), ((), ())), preferred_element_type=F32)


def kernel(
    x_hbm, wq_hbm, wo_hbm, mod_hbm, st_hbm, order_ref, qg_ref, kg_ref, time_ref,
    out_ref,
    x_in, wq, wo, mod, st_in, rows_f, st_src, gran_f,
    g0, g1, wide, xr, wmod, wodd, weven, perm, wlow, whigh, pick, colv, gatev, table, gains,
    qsrc, qrecv, stale, stale_f, keys, vals, att, ysrc, dsrc, drecv,
    load_sem, ready, nready, w_send, w_recv,
    ag_send, ag_own, ag_core,
    st_send, st_recv, q_send, q_recv,
    at_send, at_own, at_core,
    d_send, d_recv,
):
    s = lax.axis_index("section")
    p = lax.axis_index("patch")
    z = p // 4
    xl = (p // 2) % 2
    core = p % 2
    me = z * 2 + core
    after = (s + 1) % NS
    before = (s + NS - 1) % NS
    core_mate = z * 4 + xl * 2 + (1 - core)
    x_mate = z * 4 + (1 - xl) * 2 + core
    diag_mate = z * 4 + (1 - xl) * 2 + (1 - core)

    def on_line(zs, c):
        return zs * 4 + xl * 2 + c

    loads = [
        pltpu.make_async_copy(x_hbm, x_in, load_sem.at[0]),
        pltpu.make_async_copy(st_hbm.at[s], st_in.at[0], load_sem.at[1]),
        pltpu.make_async_copy(st_hbm.at[before], st_in.at[1], load_sem.at[2]),
        pltpu.make_async_copy(wq_hbm, wq.at[xl], load_sem.at[3]),
        pltpu.make_async_copy(wo_hbm, wo.at[xl], load_sem.at[4]),
        pltpu.make_async_copy(mod_hbm, mod, load_sem.at[5]),
    ]
    for load in loads:
        load.start()

    barrier = pltpu.get_barrier_semaphore()

    def greet(sec, dev):
        pl.semaphore_signal(barrier, inc=1, device_id=(sec, dev), device_id_type=MESH)

    def greet_line(i, _):
        greet(s, on_line((z + i) % NZ, core))
        return 0

    lax.fori_loop(1, NZ, greet_line, 0)
    for mate in (core_mate, x_mate, diag_mate):
        greet(s, mate)
    greet(after, p)
    greet(before, p)

    loads[0].wait()
    xf = x_in[...].astype(F32)
    for t in range(2):
        for k in range(KC):
            rows_f[pl.ds(t * KC + k, 1), :] = xf[t : t + 1, k * 128 : (k + 1) * 128]
    own = pl.ds(pl.multiple_of(me * BLK, 16), BLK)
    g0[own, :] = rows_f[...].astype(BF16)
    loads[1].wait()
    loads[2].wait()
    for tick in range(2):
        sf = st_in[tick].astype(F32)
        for kv in range(2):
            for head in range(HEADS):
                for t in range(2):
                    row = (head // 2) * 16 + (((head % 2) * 2 + tick) * 2 + kv) * 2 + t
                    low = (kv * HEADS + head) * 128
                    gran_f[pl.ds(row, 1), :] = sf[t : t + 1, low : low + 128]
    st_src[...] = gran_f[...].astype(BF16)
    for load in loads[3:]:
        load.wait()

    def block(g, b):
        return g.at[pl.ds(pl.multiple_of(b * BLK, 16), BLK)]

    def push(src, dst, send, recv, sec, dev):
        pltpu.make_async_remote_copy(
            src_ref=src, dst_ref=dst, send_sem=send, recv_sem=recv,
            device_id=(sec, dev), device_id_type=MESH,
        ).start()

    def take(ref, sem):
        pltpu.make_async_copy(ref, ref, sem).wait()

    my_pair = jnp.int32(0)
    owned = jnp.int32(0)
    for pair in range(PAIRS):
        hit = jnp.where(p == owner_of(pair, xl), 1, 0)
        my_pair = my_pair + pair * hit
        owned = owned + hit

    def finish(stage):
        if stage == 2:
            @pl.when(owned == 1)
            def _():
                take(stale, st_recv)
        if 2 <= stage < 5:
            pl.semaphore_wait(nready, 1)
        if stage >= 2:
            take(g0.at[pl.ds(0, 31 * BLK)], ag_send.at[0])
            take(wq.at[xl], w_send.at[0])
            take(wo.at[xl], w_send.at[1])

            def drain_stale(i, _):
                take(st_src.at[pl.ds(0, 16)], st_send)
                return 0

            lax.fori_loop(0, 2 * PAIRS - owned, drain_stale, 0)
        if 2 <= stage < 4:
            take(wo.at[1 - xl], w_recv.at[1])
        if stage >= 5:
            take(g1, ag_send.at[1])
        if stage >= 8:
            take(dsrc, d_send)
        mine_units = jnp.int32(0)
        for j in range(2):
            for i in range(9):
                unit = (z * 4 + 2 * j + core) * 9 + i
                pair = ((unit // 16) % HEADS) // 2
                mine_units = mine_units + jnp.where(owner_of(pair, xl) == p, 1, 0)
        for tick in range(2):
            def drain(i, _):
                take(qsrc.at[tick, 0, pl.ds(0, 8)], q_send.at[tick])
                return 0

            if stage >= 3 + 3 * tick:
                lax.fori_loop(0, 18 - mine_units, drain, 0)
            if stage >= 4 + 3 * tick:
                def drain_piece(i, _):
                    take(att.at[tick, pl.ds(0, 128)], at_send.at[tick])
                    return 0

                lax.fori_loop(0, 3 + (NZ - 1) * owned, drain_piece, 0)

    def relay_core(g, tick, zs):
        b = zs * 2 + core
        push(block(g, b), block(g, b), ag_send.at[tick], ag_core.at[tick], s, core_mate)

    def arrive(g, tick, i):
        far = (i + 1) // 2
        zs = (z + NZ - far * (2 * (i % 2) - 1)) % NZ
        take(block(g, zs * 2 + core), ag_own.at[tick, zs])
        return zs

    def near_step(g, tick):
        def step(i, _):
            relay_core(g, tick, arrive(g, tick, i))
            return 0

        return step

    def relay(g, tick, first):
        lax.fori_loop(first, 2 * REACH - 1, near_step(g, tick), 0)
        for i in (2 * REACH - 1, 2 * REACH):
            zs = arrive(g, tick, i)
            sign = 2 * (i % 2) - 1
            piece = block(g, zs * 2 + core)
            for far in range(REACH - 1 + i % 2, 0, -1):
                dev = on_line((z + NZ + sign * far) % NZ, core)
                push(piece, piece, ag_send.at[tick], ag_own.at[tick, zs], s, dev)
            relay_core(g, tick, zs)
        lax.fori_loop(2 * REACH + 1, NZ, near_step(g, tick), 0)
        take(g.at[pl.ds(0, NZ * BLK)], ag_core.at[tick])

    def spread(src, dst, tick, sec, first):
        def send(far, sign):
            dev = on_line((z + NZ + sign * far) % NZ, core)
            push(src, dst, ag_send.at[tick], ag_own.at[tick, z], sec, dev)

        send(REACH, 1)
        send(REACH, -1)
        if first == 0:
            send(0, 1)
        for far in range(1, REACH):
            send(far, 1)
            send(far, -1)

    pl.semaphore_wait(barrier, 20)

    spread(g0.at[own], g0.at[own], 0, s, 1)
    push(wq.at[xl], wq.at[xl], w_send.at[0], w_recv.at[0], s, x_mate)
    push(wo.at[xl], wo.at[xl], w_send.at[1], w_recv.at[1], s, x_mate)
    for mate in (core_mate, x_mate, diag_mate):
        pl.semaphore_signal(ready, inc=1, device_id=(s, mate), device_id_type=MESH)
    relay_core(g0, 0, z)

    times = [time_ref[s], time_ref[before]]
    lane = lax.broadcasted_iota(jnp.int32, (128, 128), 1)
    first_half = lane < 64

    def fold(tick, j):
        shift_sum = jnp.zeros((QROWS, 128), F32)
        row_sum = jnp.zeros((QROWS, 128), F32)
        base = times[tick] * 3
        for k in range(KC):
            lanes = pl.ds(k * 128, 128)
            shift = mod[base, :, lanes]
            scale = mod[base + 1, :, lanes]
            w = wq[j, :, lanes].astype(F32)
            scaled = (w * (1.0 + scale)).astype(BF16)
            wmod[tick, j, :, lanes] = scaled
            shift_sum += w * shift
            row_sum += scaled.astype(F32)
        for n, value in enumerate((shift_sum, row_sum)):
            total = jnp.sum(value, axis=1, keepdims=True)
            colv[tick, n, j] = jnp.broadcast_to(total, (QROWS, 128))

    fold(0, xl)

    pl.semaphore_wait(ready, 3)
    pl.semaphore_signal(nready, inc=1, device_id=(before, p), device_id_type=MESH)
    for pair in range(PAIRS):
        for line in range(2):
            dev = owner_of(pair, line)
            src = st_src.at[pl.ds(pair * 16, 16)]
            dst = stale.at[pl.ds(pl.multiple_of(p * 16, 16), 16)]

            @pl.when(p == dev)
            def _():
                pltpu.make_async_copy(src, dst, st_recv).start()

            @pl.when(p != dev)
            def _():
                push(src, dst, st_send, st_recv, s, dev)

    feature = lax.broadcasted_iota(jnp.int32, (BLK, 128), 1)
    row = lax.broadcasted_iota(jnp.int32, (BLK, 128), 0)
    gate_sums = []
    for j in range(2):
        mine = (z * 4 + 2 * j + core) * BLK + row
        sums = [jnp.zeros((BLK, 128), F32), jnp.zeros((BLK, 128), F32)]
        for k in range(KC):
            lanes = pl.ds(k * 128, 128)
            here = feature + k * 128 == mine
            pick[j, :, lanes] = jnp.where(here, 1.0, 0.0).astype(BF16)
            for tick in range(2):
                sums[tick] += jnp.where(here, mod[times[tick] * 3 + 2, :, lanes], 0.0)
        gate_sums.append([jnp.sum(v, axis=1, keepdims=True) for v in sums])
    for tick in range(2):
        gatev[tick] = jnp.where(first_half[:BLK], gate_sums[0][tick], gate_sums[1][tick])

    @pl.when(owned == 1)
    def _():
        r = lax.broadcasted_iota(jnp.int32, (128, 128), 0)
        for j, ref in enumerate((qg_ref, kg_ref)):
            diag = jnp.where(r == lane, jnp.broadcast_to(ref[...], (128, 128)), 0.0)
            gains[j] = jnp.broadcast_to(jnp.sum(diag, axis=1, keepdims=True), (128, 128))
        pr = r[:64]
        pc = lane[:64]
        places = jnp.broadcast_to(order_ref[...].astype(F32), (64, 64))
        column = jnp.sum(
            jnp.where(pr[:, :64] == pc[:, :64], places, 0.0), axis=1, keepdims=True
        )
        token = pc % 64
        patch = ((token % LINE) // 2) * 4 + 2 * xl + token % 2
        place = jnp.sum(jnp.where(pr == patch, column, 0.0), axis=0, keepdims=True)
        pos = place * 2.0 + jnp.where(token[:1] < LINE, 0.0, 1.0)
        freq = jnp.exp(pr.astype(F32) * (-jnp.log(F32(10000.0)) / 64.0))
        angle = pos * freq
        table[0] = jnp.cos(angle)
        table[1] = jnp.sin(angle)

    relay(g0, 0, 1)
    take(wq.at[1 - xl], w_recv.at[0])
    fold(0, 1 - xl)

    def send_qkv(tick):
        for j in range(2):
            for i in range(9):
                unit = (z * 4 + 2 * j + core) * 9 + i
                part = unit // 16
                head = part % HEADS
                dev = owner_of(head // 2, xl)
                kind = part // HEADS
                low = pl.multiple_of(kind * 128 + (unit % 16) * 8, 8)
                src = qsrc.at[tick, j, pl.ds(i * 8, 8)]
                dst = qrecv.at[tick, head % 2, pl.ds(low, 8)]

                @pl.when(p == dev)
                def _():
                    pltpu.make_async_copy(src, dst, q_recv.at[tick]).start()

                @pl.when(p != dev)
                def _():
                    push(src, dst, q_send.at[tick], q_recv.at[tick], s, dev)

    def finish_qkv(tick, accs, mean, var):
        rstd = lax.rsqrt(var + 1e-06)
        for j in range(2):
            qkv = rstd * (accs[j] - colv[tick, 1, j] * mean) + colv[tick, 0, j]
            qsrc[tick, j] = qkv.astype(BF16).astype(F32)

    for b in range(12):
        part = pl.ds(b * 128, 128)
        wide[part, :] = g0[part, :].astype(F32)
    total = jnp.zeros((64, 128), F32)
    for k in range(KC):
        lanes = pl.ds(k * 128, 128)
        piece = jnp.concatenate(
            [wide[pl.ds(t * KC + k, LINE, stride=BLK), :] for t in range(2)], axis=0
        )
        total += piece
        narrow = piece.astype(BF16)
        xr[pl.ds(0, 64), lanes] = narrow
        xr[pl.ds(64, 64), lanes] = narrow
    accs = [dot_nt(wmod[0, j], xr[...]) for j in range(2)]
    mean_c = jnp.sum(total, axis=1, keepdims=True) * (1.0 / D)
    total = jnp.zeros((64, 128), F32)
    for k in range(KC):
        centred = xr[pl.ds(0, 64), pl.ds(k * 128, 128)].astype(F32) - mean_c
        total += centred * centred
    var_c = jnp.sum(total, axis=1, keepdims=True) * (1.0 / D)
    stats = jnp.where(first_half[:64], mean_c, var_c)
    stats = jnp.transpose(jnp.concatenate([stats, stats], axis=0))
    finish_qkv(0, accs, stats[0:1, :], stats[64:65, :])
    send_qkv(0)

    @pl.when(owned == 1)
    def _():
        take(stale, st_recv)
        for b in range(8):
            part = pl.ds(b * 128, 128)
            stale_f[part, :] = stale[part, :].astype(F32)
        for tick in range(2):
            for second in range(2):
                got = []
                for kv in range(2):
                    both = [
                        stale_f[
                            pl.ds(((second * 2 + tick) * 2 + kv) * 2 + t, 64, stride=16), :
                        ]
                        for t in range(2)
                    ]
                    got.append(jnp.concatenate(both, axis=0))
                keys[tick, second] = got[0].astype(BF16)
                vals[tick, second] = jnp.transpose(got[1]).astype(BF16)

    def attend(tick):
        take(qrecv.at[tick], q_recv.at[tick])
        factor = 128.0 ** -0.5
        cosine, sine = table[0], table[1]

        def received(low):
            part = pl.ds(low, 128)
            return jnp.where(first_half, qrecv[tick, 0, part, :], qrecv[tick, 1, part, :])

        def prepared(low, j):
            u = received(low)
            square = jnp.sum(u * u, axis=0, keepdims=True) * (1.0 / 128)
            u = u * lax.rsqrt(square + 1e-06) * gains[j]
            a, b = u[:64], u[64:]
            return jnp.concatenate(
                [a * cosine - b * sine, a * sine + b * cosine], axis=0
            ).astype(BF16)

        def partner(u):
            up = pltpu.roll(u, 128 - LINE, 1)
            down = pltpu.roll(u, LINE, 1)
            return jnp.where(lane % 64 < LINE, up, down)

        query = prepared(0, 0)
        key = prepared(128, 1).astype(F32)
        value = received(256)
        scores = jnp.where(
            first_half, dot_nn(keys[tick, 0], query), dot_nn(keys[tick, 1], query)
        ) * factor
        r = lax.broadcasted_iota(jnp.int32, (128, 128), 0)
        patch = ((lane % LINE) // 2) * 4 + 2 * xl + lane % 2
        scores = jnp.where(r % 64 == patch, -1e30, scores)
        wide_q = query.astype(F32)
        same = jnp.sum(wide_q * key, axis=0, keepdims=True) * factor
        other = jnp.sum(wide_q * partner(key), axis=0, keepdims=True) * factor
        top = jnp.maximum(jnp.max(scores, axis=0, keepdims=True), jnp.maximum(same, other))
        weights = jnp.exp(scores - top)
        same = jnp.exp(same - top)
        other = jnp.exp(other - top)
        mass = jnp.sum(weights, axis=0, keepdims=True) + same + other
        weights = weights.astype(BF16)
        summed = jnp.where(
            first_half, dot_nn(vals[tick, 0], weights), dot_nn(vals[tick, 1], weights)
        )
        summed = summed + same * value + other * partner(value)
        att[tick, pair_rows(my_pair), :] = (summed / mass).astype(BF16)

    def pair_rows(pair):
        return pl.ds(pl.multiple_of(pair * 128, 128), 128)

    def send_attended(tick):
        piece = att.at[tick, pair_rows(my_pair)]

        def send(i, _):
            far = (NZ - i + 1) // 2
            dev = on_line((z + NZ + far * (2 * (i % 2) - 1)) % NZ, core)
            push(piece, piece, at_send.at[tick], at_own.at[tick, my_pair // 2], s, dev)
            return 0

        lax.fori_loop(1, NZ, send, 0)

    def gather_attended(tick):
        for j in range(3):
            pair = j * 2 + core
            piece = att.at[tick, pair_rows(pair)]

            @pl.when(owner_of(pair, xl) != p)
            def _():
                take(piece, at_own.at[tick, j])

            push(piece, piece, at_send.at[tick], at_core.at[tick], s, core_mate)
        take(att.at[tick, pl.ds(0, 3 * 128)], at_core.at[tick])

    def project(tick, residual):
        out = jnp.where(
            first_half[: 2 * BLK], dot_nn(weven[...], att[tick]), dot_nn(wodd[...], att[tick])
        )
        out = out + pltpu.roll(out, 64, 1)
        out = jnp.where(first_half[:BLK], out[:BLK], out[BLK:])
        return (residual + gatev[tick] * out).astype(BF16)

    @pl.when(owned == 1)
    def _():
        attend(0)

    @pl.when(owned == 1)
    def _():
        send_attended(0)

    picked = [dot_nt(pick[j], xr[...]) for j in range(2)]
    residual = jnp.where(first_half[:BLK], picked[0], picked[1])
    take(wo.at[1 - xl], w_recv.at[1])
    for j in range(2):
        for pair in range(PAIRS):
            at = pl.ds(j * BLK, BLK), pl.ds(pair * 128, 128)
            weven[at] = wo[j, :, pl.ds(pair * 256, 128)]
            wodd[at] = wo[j, :, pl.ds(pair * 256 + 128, 128)]
    pf = lax.broadcasted_iota(jnp.int32, (CHUNK, 128), 0)
    po = lax.broadcasted_iota(jnp.int32, (CHUNK, 128), 1)
    for k in range(CHUNK // 128):
        to = po + (k % 3) * 128
        group = jnp.where(to >= 96, 1, 0) + jnp.where(to >= 192, 1, 0) + jnp.where(to >= 288, 1, 0)
        source = to + 96 * group + 96 * (k // 3)
        perm[:, pl.ds(k * 128, 128)] = jnp.where(pf == source, 1.0, 0.0).astype(BF16)
    half = CHUNK // 2
    for j in range(2):
        fold(1, j)
        for k in range(D // CHUNK):
            moved = dot_nn(wmod[1, j, :, pl.ds(k * CHUNK, CHUNK)], perm[...]).astype(BF16)
            wlow[j, :, pl.ds(k * half, half)] = moved[:, :half]
            whigh[j, :, pl.ds(k * half, half)] = moved[:, half:]

    gather_attended(0)
    ysrc[...] = project(0, residual)

    pl.semaphore_wait(nready, 1)
    spread(ysrc, g1.at[own], 1, after, 0)

    relay(g1, 1, 0)
    accs = []
    for j in range(2):
        acc = jnp.where(
            first_half[:QROWS], dot_nn(wlow[j], g1[...]), dot_nn(whigh[j], g1[...])
        )
        accs.append(acc + pltpu.roll(acc, 64, 1))
    total = jnp.zeros((128, 128), F32)
    for k in range(12):
        total += g1[pl.ds(k * 128, 128), :].astype(F32)
    total = jnp.sum(total, axis=0, keepdims=True)
    mean = (total + pltpu.roll(total, 64, 1)) * (1.0 / D)
    total = jnp.zeros((128, 128), F32)
    for k in range(12):
        centred = g1[pl.ds(k * 128, 128), :].astype(F32) - mean
        total += centred * centred
    total = jnp.sum(total, axis=0, keepdims=True)
    var = (total + pltpu.roll(total, 64, 1)) * (1.0 / D)
    finish_qkv(1, accs, mean, var)
    send_qkv(1)

    @pl.when(owned == 1)
    def _():
        attend(1)

    @pl.when(owned == 1)
    def _():
        send_attended(1)

    gather_attended(1)
    last = project(1, g1[own, :].astype(F32)).astype(F32)
    blank = jnp.zeros((16, 128), F32)
    turned = jnp.transpose(
        jnp.concatenate([last, blank, pltpu.roll(last, 64, 1), blank], axis=0)
    )
    for i in range(LINE):
        for t in range(2):
            dsrc[i, pl.ds(t, 1), :] = turned[t * LINE + i : t * LINE + i + 1, :]

    def last_send(i, _):
        to = (me + i) % LINE
        push(dsrc.at[to], drecv.at[me], d_send, d_recv, after, on_line(to // 2, to % 2))
        return 0

    lax.fori_loop(0, LINE, last_send, 0)
    take(drecv, d_recv)
    out_ref[...] = drecv[...]
    finish(8)


def per_device(states, w_qkv, w_out, mod_table, q_gain, k_gain, stale_kv, timestep, patch_order):
    hbm = pl.BlockSpec(memory_space=pl.ANY)
    vmem = pl.BlockSpec(memory_space=pltpu.VMEM)
    dma = pltpu.SemaphoreType.DMA
    regular = pltpu.SemaphoreType.REGULAR
    got = pl.pallas_call(
        kernel,
        out_shape=jax.ShapeDtypeStruct((LINE, 2, 128), F32),
        in_specs=[hbm] * 5 + [vmem] * 3 + [pl.BlockSpec(memory_space=pltpu.SMEM)],
        out_specs=vmem,
        scratch_shapes=[
            pltpu.VMEM((2, D), BF16),
            pltpu.VMEM((2, QROWS, D), BF16),
            pltpu.VMEM((2, BLK, D // 2), BF16),
            pltpu.VMEM((84, 1, D), F32),
            pltpu.VMEM((2, 2, D), BF16),
            pltpu.VMEM((BLK, 128), F32),
            pltpu.VMEM((96, 128), BF16),
            pltpu.VMEM((96, 128), F32),
            pltpu.VMEM((LINE * BLK, 128), BF16),
            pltpu.VMEM((LINE * BLK, 128), BF16),
            pltpu.VMEM((LINE * BLK, 128), F32),
            pltpu.VMEM((128, D), BF16),
            pltpu.VMEM((2, 2, QROWS, D), BF16),
            pltpu.VMEM((2 * BLK, D // 4), BF16),
            pltpu.VMEM((2 * BLK, D // 4), BF16),
            pltpu.VMEM((CHUNK, CHUNK), BF16),
            pltpu.VMEM((2, QROWS, D // 2), BF16),
            pltpu.VMEM((2, QROWS, D // 2), BF16),
            pltpu.VMEM((2, BLK, D), BF16),
            pltpu.VMEM((2, 2, 2, QROWS, 128), F32),
            pltpu.VMEM((2, BLK, 128), F32),
            pltpu.VMEM((2, 64, 128), F32),
            pltpu.VMEM((2, 128, 128), F32),
            pltpu.VMEM((2, 2, QROWS, 128), F32),
            pltpu.VMEM((2, 2, 384, 128), F32),
            pltpu.VMEM((1024, 128), BF16),
            pltpu.VMEM((1024, 128), F32),
            pltpu.VMEM((2, 2, 128, 128), BF16),
            pltpu.VMEM((2, 2, 128, 128), BF16),
            pltpu.VMEM((2, PAIRS * 128, 128), BF16),
            pltpu.VMEM((BLK, 128), BF16),
            pltpu.VMEM((LINE, 2, 128), F32),
            pltpu.VMEM((LINE, 2, 128), F32),
            dma((6,)),
            regular,
            regular,
            dma((2,)),
            dma((2,)),
            dma((2,)),
            dma((2, NZ)),
            dma((2,)),
            dma,
            dma,
            dma((2,)),
            dma((2,)),
            dma((2,)),
            dma((2, 3)),
            dma((2,)),
            dma,
            dma,
        ],
        compiler_params=pltpu.CompilerParams(
            collective_id=0, has_side_effects=True, vmem_limit_bytes=56 * 2**20
        ),
        name="block_cycle",
    )(
        states[0],
        w_qkv[0].T,
        w_out[0].T,
        jnp.transpose(mod_table, (0, 2, 1, 3)).reshape(84, 1, D),
        stale_kv[0],
        patch_order.reshape(1, 64),
        q_gain,
        k_gain,
        timestep,
    )
    split = got.reshape(NZ, 2, 2, 2, 64)[..., :BLK]
    return jnp.transpose(split, (2, 0, 3, 1, 4)).reshape(1, 2, D).astype(BF16)


def solution(mesh):
    in_specs = (
        P("section", "patch", None),
        P("section", None, "patch"),
        P("section", None, "patch"),
        P(None, "section", None, None),
        P("section", None),
        P("section", None),
        P("section", None, "patch", None),
        P(),
        P(),
    )
    out_specs = P("section", "patch", None)
    return jax.shard_map(
        per_device, mesh=mesh, in_specs=in_specs, out_specs=out_specs, check_vma=False
    )
```

time: 121 us -> 95.2 us (0.79)
  Pallas kernels: 114 us -> 92.6 us
  local copies, waits for them, and re-layouts: 6.35 us -> 0.85 us
    pallas_call x1, Pallas kernels: 114 us -> 92.6 us  [per_device(): pl.pallas_call(kernel, out_shape=jax.ShapeDtypeStruct((LINE, 2, 128), F32...]
    unnamed x18 -> x0, local copies, waits for them, and re-layouts: 5.3 us -> none
where the time goes in v2:
time: 95.2 us; the launch traced here: 94.3 us
  Pallas kernels  92.6 us (97%)
    pallas_call x1, Pallas kernels, per_device(): pl.pallas_call(kernel, out_shape=jax.ShapeDtypeStruct((LINE, 2, 128), F32...  92.6 us

profile of v2, /device:TPU:1, one launch (start us, length us, event | category | flops | bytes accessed | tf_op | source)
XLA Modules:
  0.0 94.3 jit_solution(14542805150137744579)
XLA Ops:
  0.0 92.6 %block_cycle.1 = f32[32,2,128]{2,1,0:T(2,128)} custom-call(bf16[2,3072]{1,0:T(2,128)(2,1)} %bitcast.16, bf16[72,3072]{1,0:T(8,128)(2,1)} %bitcast.13, bf16[48,1536]{1,0:T(8,128)(2,1)} %bitcast.14, f32[84,1,3072]{2,1,0:T(1,128)} %bitcast.12, bf16[8,2,3072]{2,1,0:T(2,128)(2,1)} %bitcast.15, s32[1,64]{1,0:T(1,128)} %bitcast.17, f32[1,128]{1,0:T(1,128)} %qg_ref.1, ...), custom_call_target="tpu_custom_call" | custom-call | tf_op jit(solution)/shard_map/block_cycle/pallas_call | solution.py:550
  92.7 0.8 convert.4
  93.4 0.1 reshape.22
  93.6 0.7 convert_element_type.16
  (2 shorter events, 0.1 us)

commit v3 on v2

--- a/solution.py
+++ b/solution.py
@@ -41,7 +41,7 @@
     x_in, wq, wo, mod, st_in, rows_f, st_src, gran_f,
     g0, g1, wide, xr, wmod, wodd, weven, perm, wlow, whigh, pick, colv, gatev, table, gains,
     qsrc, qrecv, stale, stale_f, keys, vals, att, ysrc, dsrc, drecv,
-    load_sem, ready, nready, w_send, w_recv,
+    load_sem, nready, w_send, w_recv,
     ag_send, ag_own, ag_core,
     st_send, st_recv, q_send, q_recv,
     at_send, at_own, at_core,
@@ -57,7 +57,6 @@
     before = (s + NS - 1) % NS
     core_mate = z * 4 + xl * 2 + (1 - core)
     x_mate = z * 4 + (1 - xl) * 2 + core
-    diag_mate = z * 4 + (1 - xl) * 2 + (1 - core)
 
     def on_line(zs, c):
         return zs * 4 + xl * 2 + c
@@ -78,13 +77,11 @@
     def greet(sec, dev):
         pl.semaphore_signal(barrier, inc=1, device_id=(sec, dev), device_id_type=MESH)
 
-    def greet_line(i, _):
-        greet(s, on_line((z + i) % NZ, core))
-        return 0
-
-    lax.fori_loop(1, NZ, greet_line, 0)
-    for mate in (core_mate, x_mate, diag_mate):
-        greet(s, mate)
+    for far in range(1, REACH + 1):
+        greet(s, on_line((z + far) % NZ, core))
+        greet(s, on_line((z + NZ - far) % NZ, core))
+    greet(s, core_mate)
+    greet(s, x_mate)
     greet(after, p)
     greet(before, p)
 
@@ -95,20 +92,6 @@
             rows_f[pl.ds(t * KC + k, 1), :] = xf[t : t + 1, k * 128 : (k + 1) * 128]
     own = pl.ds(pl.multiple_of(me * BLK, 16), BLK)
     g0[own, :] = rows_f[...].astype(BF16)
-    loads[1].wait()
-    loads[2].wait()
-    for tick in range(2):
-        sf = st_in[tick].astype(F32)
-        for kv in range(2):
-            for head in range(HEADS):
-                for t in range(2):
-                    row = (head // 2) * 16 + (((head % 2) * 2 + tick) * 2 + kv) * 2 + t
-                    low = (kv * HEADS + head) * 128
-                    gran_f[pl.ds(row, 1), :] = sf[t : t + 1, low : low + 128]
-    st_src[...] = gran_f[...].astype(BF16)
-    for load in loads[3:]:
-        load.wait()
-
     def block(g, b):
         return g.at[pl.ds(pl.multiple_of(b * BLK, 16), BLK)]
 
@@ -129,6 +112,9 @@
         owned = owned + hit
 
     def finish(stage):
+        if stage == 1:
+            for load in loads[1:]:
+                load.wait()
         if stage == 2:
             @pl.when(owned == 1)
             def _():
@@ -138,15 +124,16 @@
         if stage >= 2:
             take(g0.at[pl.ds(0, 31 * BLK)], ag_send.at[0])
             take(wq.at[xl], w_send.at[0])
-            take(wo.at[xl], w_send.at[1])
+            take(st_src.at[0], w_send.at[1])
+            take(wo.at[xl], w_send.at[2])
 
             def drain_stale(i, _):
-                take(st_src.at[pl.ds(0, 16)], st_send)
+                take(st_src.at[0, pl.ds(0, 16)], st_send)
                 return 0
 
-            lax.fori_loop(0, 2 * PAIRS - owned, drain_stale, 0)
+            lax.fori_loop(0, 2 * (PAIRS - owned), drain_stale, 0)
         if 2 <= stage < 4:
-            take(wo.at[1 - xl], w_recv.at[1])
+            take(wo.at[1 - xl], w_recv.at[2])
         if stage >= 5:
             take(g1, ag_send.at[1])
         if stage >= 8:
@@ -214,14 +201,28 @@
             send(far, 1)
             send(far, -1)
 
-    pl.semaphore_wait(barrier, 20)
+    pl.semaphore_wait(barrier, 2 * REACH + 4)
 
     spread(g0.at[own], g0.at[own], 0, s, 1)
+    relay_core(g0, 0, z)
+    loads[3].wait()
     push(wq.at[xl], wq.at[xl], w_send.at[0], w_recv.at[0], s, x_mate)
-    push(wo.at[xl], wo.at[xl], w_send.at[1], w_recv.at[1], s, x_mate)
-    for mate in (core_mate, x_mate, diag_mate):
-        pl.semaphore_signal(ready, inc=1, device_id=(s, mate), device_id_type=MESH)
-    relay_core(g0, 0, z)
+    loads[1].wait()
+    loads[2].wait()
+    for tick in range(2):
+        sf = st_in[tick].astype(F32)
+        for kv in range(2):
+            for head in range(HEADS):
+                for t in range(2):
+                    row = (head // 2) * 16 + (((head % 2) * 2 + tick) * 2 + kv) * 2 + t
+                    low = (kv * HEADS + head) * 128
+                    gran_f[pl.ds(row, 1), :] = sf[t : t + 1, low : low + 128]
+    st_src[0] = gran_f[...].astype(BF16)
+    push(st_src.at[0], st_src.at[1], w_send.at[1], w_recv.at[1], s, x_mate)
+    loads[4].wait()
+    push(wo.at[xl], wo.at[xl], w_send.at[2], w_recv.at[2], s, x_mate)
+    loads[5].wait()
+
 
     times = [time_ref[s], time_ref[before]]
     lane = lax.broadcasted_iota(jnp.int32, (128, 128), 1)
@@ -245,22 +246,6 @@
             colv[tick, n, j] = jnp.broadcast_to(total, (QROWS, 128))
 
     fold(0, xl)
-
-    pl.semaphore_wait(ready, 3)
-    pl.semaphore_signal(nready, inc=1, device_id=(before, p), device_id_type=MESH)
-    for pair in range(PAIRS):
-        for line in range(2):
-            dev = owner_of(pair, line)
-            src = st_src.at[pl.ds(pair * 16, 16)]
-            dst = stale.at[pl.ds(pl.multiple_of(p * 16, 16), 16)]
-
-            @pl.when(p == dev)
-            def _():
-                pltpu.make_async_copy(src, dst, st_recv).start()
-
-            @pl.when(p != dev)
-            def _():
-                push(src, dst, st_send, st_recv, s, dev)
 
     feature = lax.broadcasted_iota(jnp.int32, (BLK, 128), 1)
     row = lax.broadcasted_iota(jnp.int32, (BLK, 128), 0)
@@ -300,6 +285,24 @@
         table[1] = jnp.sin(angle)
 
     relay(g0, 0, 1)
+    pl.semaphore_signal(nready, inc=1, device_id=(before, p), device_id_type=MESH)
+
+    take(st_src.at[1], w_recv.at[1])
+    for pair in range(PAIRS):
+        dev = owner_of(pair, xl)
+        for j in range(2):
+            src = st_src.at[j, pl.ds(pair * 16, 16)]
+            origin = z * 4 + 2 * (xl if j == 0 else 1 - xl) + core
+            dst = stale.at[pl.ds(pl.multiple_of(origin * 16, 16), 16)]
+
+            @pl.when(p == dev)
+            def _():
+                pltpu.make_async_copy(src, dst, st_recv).start()
+
+            @pl.when(p != dev)
+            def _():
+                push(src, dst, st_send, st_recv, s, dev)
+
     take(wq.at[1 - xl], w_recv.at[0])
     fold(0, 1 - xl)
 
@@ -465,7 +468,7 @@
 
     picked = [dot_nt(pick[j], xr[...]) for j in range(2)]
     residual = jnp.where(first_half[:BLK], picked[0], picked[1])
-    take(wo.at[1 - xl], w_recv.at[1])
+    take(wo.at[1 - xl], w_recv.at[2])
     for j in range(2):
         for pair in range(PAIRS):
             at = pl.ds(j * BLK, BLK), pl.ds(pair * 128, 128)
@@ -559,7 +562,7 @@
             pltpu.VMEM((84, 1, D), F32),
             pltpu.VMEM((2, 2, D), BF16),
             pltpu.VMEM((BLK, 128), F32),
-            pltpu.VMEM((96, 128), BF16),
+            pltpu.VMEM((2, 96, 128), BF16),
             pltpu.VMEM((96, 128), F32),
             pltpu.VMEM((LINE * BLK, 128), BF16),
             pltpu.VMEM((LINE * BLK, 128), BF16),
@@ -588,9 +591,8 @@
             pltpu.VMEM((LINE, 2, 128), F32),
             dma((6,)),
             regular,
-            regular,
-            dma((2,)),
-            dma((2,)),
+            dma((3,)),
+            dma((3,)),
             dma((2,)),
             dma((2, NZ)),
             dma((2,)),

time: 95.2 us -> 95.8 us (level)
  Pallas kernels: 92.6 us -> 94 us
    pallas_call x1, Pallas kernels: 92.6 us -> 94 us  [per_device(): pl.pallas_call(kernel, out_shape=jax.ShapeDtypeStruct((LINE, 2, 128), F32...]
where the time goes in v3:
time: 95.8 us; the launch traced here: 95.6 us
  Pallas kernels  94 us (98%)
    pallas_call x1, Pallas kernels, per_device(): pl.pallas_call(kernel, out_shape=jax.ShapeDtypeStruct((LINE, 2, 128), F32...  94 us

profile of v3, /device:TPU:1, one launch (start us, length us, event | category | flops | bytes accessed | tf_op | source)
XLA Modules:
  0.0 95.6 jit_solution(11457629306811271887)
XLA Ops:
  0.0 94.0 %block_cycle.1 = f32[32,2,128]{2,1,0:T(2,128)} custom-call(bf16[2,3072]{1,0:T(2,128)(2,1)} %bitcast.16, bf16[72,3072]{1,0:T(8,128)(2,1)} %bitcast.13, bf16[48,1536]{1,0:T(8,128)(2,1)} %bitcast.14, f32[84,1,3072]{2,1,0:T(1,128)} %bitcast.12, bf16[8,2,3072]{2,1,0:T(2,128)(2,1)} %bitcast.15, s32[1,64]{1,0:T(1,128)} %bitcast.17, f32[1,128]{1,0:T(1,128)} %qg_ref.1, ...), custom_call_target="tpu_custom_call" | custom-call | tf_op jit(solution)/shard_map/block_cycle/pallas_call | solution.py:553
  94.0 0.8 convert.4
  94.7 0.1 reshape.22
  94.9 0.7 convert_element_type.16
  (2 shorter events, 0.1 us)

commit v4 on v3

--- a/solution.py
+++ b/solution.py
@@ -38,9 +38,9 @@
 def kernel(
     x_hbm, wq_hbm, wo_hbm, mod_hbm, st_hbm, order_ref, qg_ref, kg_ref, time_ref,
     out_ref,
-    x_in, wq, wo, mod, st_in, rows_f, st_src, gran_f,
+    x_in, wq, wo, mod, st_in, rows_f, st_src, st_own, st_mate, gran_f,
     g0, g1, wide, xr, wmod, wodd, weven, perm, wlow, whigh, pick, colv, gatev, table, gains,
-    qsrc, qrecv, stale, stale_f, keys, vals, att, ysrc, dsrc, drecv,
+    qsrc, qrecv, merged, stale, stale_f, keys, vals, att, ysrc, dsrc, drecv,
     load_sem, nready, w_send, w_recv,
     ag_send, ag_own, ag_core,
     st_send, st_recv, q_send, q_recv,
@@ -111,6 +111,13 @@
         my_pair = my_pair + pair * hit
         owned = owned + hit
 
+    def drain_stale(tick):
+        def step(i, _):
+            take(st_src.at[tick, pl.ds(0, 16)], st_send.at[tick])
+            return 0
+
+        lax.fori_loop(0, PAIRS - owned, step, 0)
+
     def finish(stage):
         if stage == 1:
             for load in loads[1:]:
@@ -118,22 +125,25 @@
         if stage == 2:
             @pl.when(owned == 1)
             def _():
-                take(stale, st_recv)
+                take(stale.at[0], st_recv.at[0])
+            take(wq.at[1 - xl], w_recv.at[0])
+        if 3 <= stage < 6:
+            @pl.when(owned == 1)
+            def _():
+                take(stale.at[1], st_recv.at[1])
         if 2 <= stage < 5:
             pl.semaphore_wait(nready, 1)
         if stage >= 2:
             take(g0.at[pl.ds(0, 31 * BLK)], ag_send.at[0])
             take(wq.at[xl], w_send.at[0])
-            take(st_src.at[0], w_send.at[1])
             take(wo.at[xl], w_send.at[2])
 
-            def drain_stale(i, _):
-                take(st_src.at[0, pl.ds(0, 16)], st_send)
-                return 0
-
-            lax.fori_loop(0, 2 * (PAIRS - owned), drain_stale, 0)
+            drain_stale(0)
+            take(st_own, w_send.at[1])
         if 2 <= stage < 4:
             take(wo.at[1 - xl], w_recv.at[2])
+        if stage >= 3:
+            drain_stale(1)
         if stage >= 5:
             take(g1, ag_send.at[1])
         if stage >= 8:
@@ -146,7 +156,7 @@
                 mine_units = mine_units + jnp.where(owner_of(pair, xl) == p, 1, 0)
         for tick in range(2):
             def drain(i, _):
-                take(qsrc.at[tick, 0, pl.ds(0, 8)], q_send.at[tick])
+                take(qsrc.at[tick, 0, 0], q_send.at[tick])
                 return 0
 
             if stage >= 3 + 3 * tick:
@@ -214,11 +224,11 @@
         for kv in range(2):
             for head in range(HEADS):
                 for t in range(2):
-                    row = (head // 2) * 16 + (((head % 2) * 2 + tick) * 2 + kv) * 2 + t
+                    row = tick * 48 + (head // 2) * 8 + ((head % 2) * 2 + kv) * 2 + t
                     low = (kv * HEADS + head) * 128
                     gran_f[pl.ds(row, 1), :] = sf[t : t + 1, low : low + 128]
-    st_src[0] = gran_f[...].astype(BF16)
-    push(st_src.at[0], st_src.at[1], w_send.at[1], w_recv.at[1], s, x_mate)
+    st_own[...] = gran_f[...].astype(BF16)
+    push(st_own, st_mate, w_send.at[1], w_recv.at[1], s, x_mate)
     loads[4].wait()
     push(wo.at[xl], wo.at[xl], w_send.at[2], w_recv.at[2], s, x_mate)
     loads[5].wait()
@@ -287,50 +297,54 @@
     relay(g0, 0, 1)
     pl.semaphore_signal(nready, inc=1, device_id=(before, p), device_id_type=MESH)
 
-    take(st_src.at[1], w_recv.at[1])
-    for pair in range(PAIRS):
-        dev = owner_of(pair, xl)
-        for j in range(2):
-            src = st_src.at[j, pl.ds(pair * 16, 16)]
-            origin = z * 4 + 2 * (xl if j == 0 else 1 - xl) + core
-            dst = stale.at[pl.ds(pl.multiple_of(origin * 16, 16), 16)]
+    def send_stale(tick):
+        for pair in range(PAIRS):
+            dev = owner_of(pair, xl)
+            src = st_src.at[tick, pl.ds(pair * 16, 16)]
+            dst = stale.at[tick, pl.ds(pl.multiple_of(me * 16, 16), 16)]
 
             @pl.when(p == dev)
             def _():
-                pltpu.make_async_copy(src, dst, st_recv).start()
+                pltpu.make_async_copy(src, dst, st_recv.at[tick]).start()
 
             @pl.when(p != dev)
             def _():
-                push(src, dst, st_send, st_recv, s, dev)
-
-    take(wq.at[1 - xl], w_recv.at[0])
-    fold(0, 1 - xl)
-
-    def send_qkv(tick):
-        for j in range(2):
-            for i in range(9):
-                unit = (z * 4 + 2 * j + core) * 9 + i
-                part = unit // 16
-                head = part % HEADS
-                dev = owner_of(head // 2, xl)
-                kind = part // HEADS
-                low = pl.multiple_of(kind * 128 + (unit % 16) * 8, 8)
-                src = qsrc.at[tick, j, pl.ds(i * 8, 8)]
-                dst = qrecv.at[tick, head % 2, pl.ds(low, 8)]
-
-                @pl.when(p == dev)
-                def _():
-                    pltpu.make_async_copy(src, dst, q_recv.at[tick]).start()
-
-                @pl.when(p != dev)
-                def _():
-                    push(src, dst, q_send.at[tick], q_recv.at[tick], s, dev)
-
-    def finish_qkv(tick, accs, mean, var):
-        rstd = lax.rsqrt(var + 1e-06)
-        for j in range(2):
-            qkv = rstd * (accs[j] - colv[tick, 1, j] * mean) + colv[tick, 0, j]
-            qsrc[tick, j] = qkv.astype(BF16).astype(F32)
+                push(src, dst, st_send.at[tick], st_recv.at[tick], s, dev)
+
+    take(st_mate, w_recv.at[1])
+    other_f = st_mate[...].astype(F32)
+    own_f = gran_f[...]
+    low_f = jnp.where(xl == 0, own_f, other_f)
+    high_f = jnp.where(xl == 0, other_f, own_f)
+    for tick in range(2):
+        for pair in range(PAIRS):
+            low = tick * 48 + pair * 8
+            both = jnp.concatenate([low_f[low : low + 8], high_f[low : low + 8]], axis=0)
+            st_src[tick, pl.ds(pair * 16, 16), :] = both.astype(BF16)
+    send_stale(0)
+
+
+    def send_qkv(tick, j, acc, mean, var):
+        qkv = lax.rsqrt(var + 1e-06) * (acc - colv[tick, 1, j] * mean) + colv[tick, 0, j]
+        qkv = qkv.astype(BF16).astype(F32)
+        for i in range(9):
+            top, bottom = qkv[i * 8 : i * 8 + 4], qkv[i * 8 + 4 : i * 8 + 8]
+            qsrc[tick, j, i] = jnp.where(first_half[:4], top, bottom)
+        for i in range(9):
+            unit = (z * 4 + 2 * j + core) * 9 + i
+            part = unit // 16
+            head = part % HEADS
+            dev = owner_of(head // 2, xl)
+            src = qsrc.at[tick, j, i]
+            dst = qrecv.at[tick, head % 2, (part // HEADS) * 16 + unit % 16]
+
+            @pl.when(p == dev)
+            def _():
+                pltpu.make_async_copy(src, dst, q_recv.at[tick]).start()
+
+            @pl.when(p != dev)
+            def _():
+                push(src, dst, q_send.at[tick], q_recv.at[tick], s, dev)
 
     for b in range(12):
         part = pl.ds(b * 128, 128)
@@ -345,7 +359,7 @@
         narrow = piece.astype(BF16)
         xr[pl.ds(0, 64), lanes] = narrow
         xr[pl.ds(64, 64), lanes] = narrow
-    accs = [dot_nt(wmod[0, j], xr[...]) for j in range(2)]
+    acc_own = dot_nt(wmod[0, xl], xr[...])
     mean_c = jnp.sum(total, axis=1, keepdims=True) * (1.0 / D)
     total = jnp.zeros((64, 128), F32)
     for k in range(KC):
@@ -354,40 +368,53 @@
     var_c = jnp.sum(total, axis=1, keepdims=True) * (1.0 / D)
     stats = jnp.where(first_half[:64], mean_c, var_c)
     stats = jnp.transpose(jnp.concatenate([stats, stats], axis=0))
-    finish_qkv(0, accs, stats[0:1, :], stats[64:65, :])
-    send_qkv(0)
+    mean0, var0 = stats[0:1, :], stats[64:65, :]
+    send_qkv(0, xl, acc_own, mean0, var0)
+    take(wq.at[1 - xl], w_recv.at[0])
+    fold(0, 1 - xl)
+    send_qkv(0, 1 - xl, dot_nt(wmod[0, 1 - xl], xr[...]), mean0, var0)
+    send_stale(1)
+
+    def unpack_stale(tick):
+        take(stale.at[tick], st_recv.at[tick])
+        for b in range(4):
+            part = pl.ds(b * 128, 128)
+            stale_f[part, :] = stale[tick, part, :].astype(F32)
+        for second in range(2):
+            got = []
+            for kv in range(2):
+                pieces = [
+                    stale_f[pl.ds(line * 8 + (second * 2 + kv) * 2 + t, LINE, stride=16), :]
+                    for t in range(2)
+                    for line in range(2)
+                ]
+                got.append(jnp.concatenate(pieces, axis=0))
+            keys[tick, second] = got[0].astype(BF16)
+            vals[tick, second] = jnp.transpose(got[1]).astype(BF16)
 
     @pl.when(owned == 1)
     def _():
-        take(stale, st_recv)
-        for b in range(8):
-            part = pl.ds(b * 128, 128)
-            stale_f[part, :] = stale[part, :].astype(F32)
-        for tick in range(2):
-            for second in range(2):
-                got = []
-                for kv in range(2):
-                    both = [
-                        stale_f[
-                            pl.ds(((second * 2 + tick) * 2 + kv) * 2 + t, 64, stride=16), :
-                        ]
-                        for t in range(2)
-                    ]
-                    got.append(jnp.concatenate(both, axis=0))
-                keys[tick, second] = got[0].astype(BF16)
-                vals[tick, second] = jnp.transpose(got[1]).astype(BF16)
+        unpack_stale(0)
 
     def attend(tick):
         take(qrecv.at[tick], q_recv.at[tick])
         factor = 128.0 ** -0.5
         cosine, sine = table[0], table[1]
 
-        def received(low):
-            part = pl.ds(low, 128)
-            return jnp.where(first_half, qrecv[tick, 0, part, :], qrecv[tick, 1, part, :])
-
-        def prepared(low, j):
-            u = received(low)
+        def received(kind):
+            left = first_half[:4]
+            for i in range(16):
+                first, second = qrecv[tick, 0, kind * 16 + i], qrecv[tick, 1, kind * 16 + i]
+                merged[kind, pl.ds(i * 8, 4), :] = jnp.where(
+                    left, first, pltpu.roll(second, 64, 1)
+                )
+                merged[kind, pl.ds(i * 8 + 4, 4), :] = jnp.where(
+                    left, pltpu.roll(first, 64, 1), second
+                )
+            return merged[kind]
+
+        def prepared(j):
+            u = received(j)
             square = jnp.sum(u * u, axis=0, keepdims=True) * (1.0 / 128)
             u = u * lax.rsqrt(square + 1e-06) * gains[j]
             a, b = u[:64], u[64:]
@@ -400,15 +427,16 @@
             down = pltpu.roll(u, LINE, 1)
             return jnp.where(lane % 64 < LINE, up, down)
 
-        query = prepared(0, 0)
-        key = prepared(128, 1).astype(F32)
-        value = received(256)
+        query = prepared(0)
+        key = prepared(1).astype(F32)
+        value = received(2)
         scores = jnp.where(
             first_half, dot_nn(keys[tick, 0], query), dot_nn(keys[tick, 1], query)
         ) * factor
         r = lax.broadcasted_iota(jnp.int32, (128, 128), 0)
-        patch = ((lane % LINE) // 2) * 4 + 2 * xl + lane % 2
-        scores = jnp.where(r % 64 == patch, -1e30, scores)
+        key_line = (r // LINE) % 2
+        own_patch = (r % LINE == lane % LINE) & (key_line == xl)
+        scores = jnp.where(own_patch, -1e30, scores)
         wide_q = query.astype(F32)
         same = jnp.sum(wide_q * key, axis=0, keepdims=True) * factor
         other = jnp.sum(wide_q * partner(key), axis=0, keepdims=True) * factor
@@ -513,11 +541,12 @@
         total += centred * centred
     total = jnp.sum(total, axis=0, keepdims=True)
     var = (total + pltpu.roll(total, 64, 1)) * (1.0 / D)
-    finish_qkv(1, accs, mean, var)
-    send_qkv(1)
+    for j in range(2):
+        send_qkv(1, j, accs[j], mean, var)
 
     @pl.when(owned == 1)
     def _():
+        unpack_stale(1)
         attend(1)
 
     @pl.when(owned == 1)
@@ -563,6 +592,8 @@
             pltpu.VMEM((2, 2, D), BF16),
             pltpu.VMEM((BLK, 128), F32),
             pltpu.VMEM((2, 96, 128), BF16),
+            pltpu.VMEM((96, 128), BF16),
+            pltpu.VMEM((96, 128), BF16),
             pltpu.VMEM((96, 128), F32),
             pltpu.VMEM((LINE * BLK, 128), BF16),
             pltpu.VMEM((LINE * BLK, 128), BF16),
@@ -579,10 +610,11 @@
             pltpu.VMEM((2, BLK, 128), F32),
             pltpu.VMEM((2, 64, 128), F32),
             pltpu.VMEM((2, 128, 128), F32),
-            pltpu.VMEM((2, 2, QROWS, 128), F32),
-            pltpu.VMEM((2, 2, 384, 128), F32),
-            pltpu.VMEM((1024, 128), BF16),
-            pltpu.VMEM((1024, 128), F32),
+            pltpu.VMEM((2, 2, 9, 4, 128), F32),
+            pltpu.VMEM((2, 2, 48, 4, 128), F32),
+            pltpu.VMEM((3, 128, 128), F32),
+            pltpu.VMEM((2, 512, 128), BF16),
+            pltpu.VMEM((512, 128), F32),
             pltpu.VMEM((2, 2, 128, 128), BF16),
             pltpu.VMEM((2, 2, 128, 128), BF16),
             pltpu.VMEM((2, PAIRS * 128, 128), BF16),
@@ -596,8 +628,8 @@
             dma((2,)),
             dma((2, NZ)),
             dma((2,)),
-            dma,
-            dma,
+            dma((2,)),
+            dma((2,)),
             dma((2,)),
             dma((2,)),
             dma((2,)),

time: 95.8 us -> 92.7 us (0.968)
  Pallas kernels: 94 us -> 90.9 us
    pallas_call x1, Pallas kernels: 94 us -> 90.9 us  [per_device(): pl.pallas_call(kernel, out_shape=jax.ShapeDtypeStruct((LINE, 2, 128), F32...]
where the time goes in v4:
time: 92.7 us; the launch traced here: 92.5 us
  Pallas kernels  90.9 us (98%)
    pallas_call x1, Pallas kernels, per_device(): pl.pallas_call(kernel, out_shape=jax.ShapeDtypeStruct((LINE, 2, 128), F32...  90.9 us

profile of v4, /device:TPU:1, one launch (start us, length us, event | category | flops | bytes accessed | tf_op | source)
XLA Modules:
  0.0 92.5 jit_solution(16214516152449109494)
XLA Ops:
  0.0 90.9 %block_cycle.1 = f32[32,2,128]{2,1,0:T(2,128)} custom-call(bf16[2,3072]{1,0:T(2,128)(2,1)} %bitcast.16, bf16[72,3072]{1,0:T(8,128)(2,1)} %bitcast.13, bf16[48,1536]{1,0:T(8,128)(2,1)} %bitcast.14, f32[84,1,3072]{2,1,0:T(1,128)} %bitcast.12, bf16[8,2,3072]{2,1,0:T(2,128)(2,1)} %bitcast.15, s32[1,64]{1,0:T(1,128)} %bitcast.17, f32[1,128]{1,0:T(1,128)} %qg_ref.1, ...), custom_call_target="tpu_custom_call" | custom-call | tf_op jit(solution)/shard_map/block_cycle/pallas_call | solution.py:582
  90.9 0.8 convert.4
  91.7 0.1 reshape.22
  91.8 0.7 convert_element_type.16
  (2 shorter events, 0.1 us)

commit v5 on v4

--- a/solution.py
+++ b/solution.py
@@ -39,7 +39,7 @@
     x_hbm, wq_hbm, wo_hbm, mod_hbm, st_hbm, order_ref, qg_ref, kg_ref, time_ref,
     out_ref,
     x_in, wq, wo, mod, st_in, rows_f, st_src, st_own, st_mate, gran_f,
-    g0, g1, wide, xr, wmod, wodd, weven, perm, wlow, whigh, pick, colv, gatev, table, gains,
+    g0, g1, wide, xr, wmod, wodd, weven, perm, wline, pick, colv, gatev, table, gains,
     qsrc, qrecv, merged, stale, stale_f, keys, vals, att, ysrc, dsrc, drecv,
     load_sem, nready, w_send, w_recv,
     ag_send, ag_own, ag_core,
@@ -104,6 +104,15 @@
     def take(ref, sem):
         pltpu.make_async_copy(ref, ref, sem).wait()
 
+    routes = []
+    for j in range(2):
+        for i in range(9):
+            unit = (z * 4 + 2 * j + core) * 9 + i
+            part = unit // 16
+            head = part % HEADS
+            dev = owner_of(head // 2, xl)
+            routes.append((dev, head % 2, (part // HEADS) * 16 + unit % 16))
+
     my_pair = jnp.int32(0)
     owned = jnp.int32(0)
     for pair in range(PAIRS):
@@ -120,7 +129,7 @@
 
     def finish(stage):
         if stage == 1:
-            for load in loads[1:]:
+            for load in loads[4:]:
                 load.wait()
         if stage == 2:
             @pl.when(owned == 1)
@@ -149,11 +158,8 @@
         if stage >= 8:
             take(dsrc, d_send)
         mine_units = jnp.int32(0)
-        for j in range(2):
-            for i in range(9):
-                unit = (z * 4 + 2 * j + core) * 9 + i
-                pair = ((unit // 16) % HEADS) // 2
-                mine_units = mine_units + jnp.where(owner_of(pair, xl) == p, 1, 0)
+        for dev, _, _ in routes:
+            mine_units = mine_units + jnp.where(dev == p, 1, 0)
         for tick in range(2):
             def drain(i, _):
                 take(qsrc.at[tick, 0, 0], q_send.at[tick])
@@ -185,16 +191,21 @@
 
         return step
 
-    def relay(g, tick, first):
-        lax.fori_loop(first, 2 * REACH - 1, near_step(g, tick), 0)
+    def relay(g, tick, first, between=None):
+        edge = []
         for i in (2 * REACH - 1, 2 * REACH):
             zs = arrive(g, tick, i)
+            edge.append(zs)
             sign = 2 * (i % 2) - 1
             piece = block(g, zs * 2 + core)
             for far in range(REACH - 1 + i % 2, 0, -1):
                 dev = on_line((z + NZ + sign * far) % NZ, core)
                 push(piece, piece, ag_send.at[tick], ag_own.at[tick, zs], s, dev)
+        lax.fori_loop(first, 2 * REACH - 1, near_step(g, tick), 0)
+        for zs in edge:
             relay_core(g, tick, zs)
+        if between is not None:
+            between()
         lax.fori_loop(2 * REACH + 1, NZ, near_step(g, tick), 0)
         take(g.at[pl.ds(0, NZ * BLK)], ag_core.at[tick])
 
@@ -205,18 +216,12 @@
 
         send(REACH, 1)
         send(REACH, -1)
+        for far in range(REACH - 1, 0, -1):
+            send(far, 1)
+            send(far, -1)
         if first == 0:
             send(0, 1)
-        for far in range(1, REACH):
-            send(far, 1)
-            send(far, -1)
-
-    pl.semaphore_wait(barrier, 2 * REACH + 4)
-
-    spread(g0.at[own], g0.at[own], 0, s, 1)
-    relay_core(g0, 0, z)
-    loads[3].wait()
-    push(wq.at[xl], wq.at[xl], w_send.at[0], w_recv.at[0], s, x_mate)
+
     loads[1].wait()
     loads[2].wait()
     for tick in range(2):
@@ -228,9 +233,15 @@
                     low = (kv * HEADS + head) * 128
                     gran_f[pl.ds(row, 1), :] = sf[t : t + 1, low : low + 128]
     st_own[...] = gran_f[...].astype(BF16)
+    loads[3].wait()
+
+    pl.semaphore_wait(barrier, 2 * REACH + 4)
+
+    spread(g0.at[own], g0.at[own], 0, s, 1)
+    relay_core(g0, 0, z)
     push(st_own, st_mate, w_send.at[1], w_recv.at[1], s, x_mate)
+    push(wq.at[xl], wq.at[xl], w_send.at[0], w_recv.at[0], s, x_mate)
     loads[4].wait()
-    push(wo.at[xl], wo.at[xl], w_send.at[2], w_recv.at[2], s, x_mate)
     loads[5].wait()
 
 
@@ -294,7 +305,19 @@
         table[0] = jnp.cos(angle)
         table[1] = jnp.sin(angle)
 
-    relay(g0, 0, 1)
+    def build_stale():
+        take(st_mate, w_recv.at[1])
+        other_f = st_mate[...].astype(F32)
+        own_f = gran_f[...]
+        low_f = jnp.where(xl == 0, own_f, other_f)
+        high_f = jnp.where(xl == 0, other_f, own_f)
+        for tick in range(2):
+            for pair in range(PAIRS):
+                low = tick * 48 + pair * 8
+                both = jnp.concatenate([low_f[low : low + 8], high_f[low : low + 8]], axis=0)
+                st_src[tick, pl.ds(pair * 16, 16), :] = both.astype(BF16)
+
+    relay(g0, 0, 1, build_stale)
     pl.semaphore_signal(nready, inc=1, device_id=(before, p), device_id_type=MESH)
 
     def send_stale(tick):
@@ -311,32 +334,25 @@
             def _():
                 push(src, dst, st_send.at[tick], st_recv.at[tick], s, dev)
 
-    take(st_mate, w_recv.at[1])
-    other_f = st_mate[...].astype(F32)
-    own_f = gran_f[...]
-    low_f = jnp.where(xl == 0, own_f, other_f)
-    high_f = jnp.where(xl == 0, other_f, own_f)
-    for tick in range(2):
-        for pair in range(PAIRS):
-            low = tick * 48 + pair * 8
-            both = jnp.concatenate([low_f[low : low + 8], high_f[low : low + 8]], axis=0)
-            st_src[tick, pl.ds(pair * 16, 16), :] = both.astype(BF16)
     send_stale(0)
 
 
     def send_qkv(tick, j, acc, mean, var):
+        static = isinstance(j, int)
         qkv = lax.rsqrt(var + 1e-06) * (acc - colv[tick, 1, j] * mean) + colv[tick, 0, j]
         qkv = qkv.astype(BF16).astype(F32)
         for i in range(9):
             top, bottom = qkv[i * 8 : i * 8 + 4], qkv[i * 8 + 4 : i * 8 + 8]
             qsrc[tick, j, i] = jnp.where(first_half[:4], top, bottom)
         for i in range(9):
-            unit = (z * 4 + 2 * j + core) * 9 + i
-            part = unit // 16
-            head = part % HEADS
-            dev = owner_of(head // 2, xl)
+            if static:
+                dev, half, slot = routes[j * 9 + i]
+            else:
+                dev, half, slot = [
+                    jnp.where(j == 0, a, b) for a, b in zip(routes[i], routes[9 + i])
+                ]
             src = qsrc.at[tick, j, i]
-            dst = qrecv.at[tick, head % 2, (part // HEADS) * 16 + unit % 16]
+            dst = qrecv.at[tick, half, slot]
 
             @pl.when(p == dev)
             def _():
@@ -371,6 +387,7 @@
     mean0, var0 = stats[0:1, :], stats[64:65, :]
     send_qkv(0, xl, acc_own, mean0, var0)
     take(wq.at[1 - xl], w_recv.at[0])
+    push(wo.at[xl], wo.at[xl], w_send.at[2], w_recv.at[2], s, x_mate)
     fold(0, 1 - xl)
     send_qkv(0, 1 - xl, dot_nt(wmod[0, 1 - xl], xr[...]), mean0, var0)
     send_stale(1)
@@ -513,9 +530,11 @@
     for j in range(2):
         fold(1, j)
         for k in range(D // CHUNK):
-            moved = dot_nn(wmod[1, j, :, pl.ds(k * CHUNK, CHUNK)], perm[...]).astype(BF16)
-            wlow[j, :, pl.ds(k * half, half)] = moved[:, :half]
-            whigh[j, :, pl.ds(k * half, half)] = moved[:, half:]
+            moved = dot_nn(wmod[1, j, :, pl.ds(k * CHUNK, CHUNK)], perm[...])
+            moved = jnp.concatenate([moved, jnp.zeros((8, CHUNK), F32)], axis=0).astype(BF16)
+            lanes = pl.ds(k * half, half)
+            wline[pl.ds(j * 160, 80), lanes] = moved[:, :half]
+            wline[pl.ds(j * 160 + 80, 80), lanes] = moved[:, half:]
 
     gather_attended(0)
     ysrc[...] = project(0, residual)
@@ -524,11 +543,11 @@
     spread(ysrc, g1.at[own], 1, after, 0)
 
     relay(g1, 1, 0)
+    product = dot_nn(wline[...], g1[...])
     accs = []
     for j in range(2):
-        acc = jnp.where(
-            first_half[:QROWS], dot_nn(wlow[j], g1[...]), dot_nn(whigh[j], g1[...])
-        )
+        low, high = product[j * 160 : j * 160 + QROWS], product[j * 160 + 80 : j * 160 + 80 + QROWS]
+        acc = jnp.where(first_half[:QROWS], low, high)
         accs.append(acc + pltpu.roll(acc, 64, 1))
     total = jnp.zeros((128, 128), F32)
     for k in range(12):
@@ -564,7 +583,7 @@
             dsrc[i, pl.ds(t, 1), :] = turned[t * LINE + i : t * LINE + i + 1, :]
 
     def last_send(i, _):
-        to = (me + i) % LINE
+        to = (me + LINE // 2 + LINE + (i + 1) // 2 * (2 * (i % 2) - 1)) % LINE
         push(dsrc.at[to], drecv.at[me], d_send, d_recv, after, on_line(to // 2, to % 2))
         return 0
 
@@ -603,8 +622,7 @@
             pltpu.VMEM((2 * BLK, D // 4), BF16),
             pltpu.VMEM((2 * BLK, D // 4), BF16),
             pltpu.VMEM((CHUNK, CHUNK), BF16),
-            pltpu.VMEM((2, QROWS, D // 2), BF16),
-            pltpu.VMEM((2, QROWS, D // 2), BF16),
+            pltpu.VMEM((320, D // 2), BF16),
             pltpu.VMEM((2, BLK, D), BF16),
             pltpu.VMEM((2, 2, 2, QROWS, 128), F32),
             pltpu.VMEM((2, BLK, 128), F32),

time: 92.7 us -> 87.8 us (0.947)
  Pallas kernels: 90.9 us -> 86 us
    pallas_call x1, Pallas kernels: 90.9 us -> 86 us  [per_device(): pl.pallas_call(kernel, out_shape=jax.ShapeDtypeStruct((LINE, 2, 128), F32...]
where the time goes in v5:
time: 87.8 us; the launch traced here: 87.6 us
  Pallas kernels  86 us (98%)
    pallas_call x1, Pallas kernels, per_device(): pl.pallas_call(kernel, out_shape=jax.ShapeDtypeStruct((LINE, 2, 128), F32...  86 us

profile of v5, /device:TPU:1, one launch (start us, length us, event | category | flops | bytes accessed | tf_op | source)
XLA Modules:
  0.0 87.6 jit_solution(11210424295342381930)
XLA Ops:
  0.0 86.0 %block_cycle.1 = f32[32,2,128]{2,1,0:T(2,128)} custom-call(bf16[2,3072]{1,0:T(2,128)(2,1)} %bitcast.16, bf16[72,3072]{1,0:T(8,128)(2,1)} %bitcast.13, bf16[48,1536]{1,0:T(8,128)(2,1)} %bitcast.14, f32[84,1,3072]{2,1,0:T(1,128)} %bitcast.12, bf16[8,2,3072]{2,1,0:T(2,128)(2,1)} %bitcast.15, s32[1,64]{1,0:T(1,128)} %bitcast.17, f32[1,128]{1,0:T(1,128)} %qg_ref.1, ...), custom_call_target="tpu_custom_call" | custom-call | tf_op jit(solution)/shard_map/block_cycle/pallas_call | solution.py:601
  86.0 0.8 convert.4
  86.7 0.1 reshape.22
  86.9 0.7 convert_element_type.16
  (2 shorter events, 0.1 us)

commit v6 on v5

--- a/solution.py
+++ b/solution.py
@@ -39,7 +39,7 @@
     x_hbm, wq_hbm, wo_hbm, mod_hbm, st_hbm, order_ref, qg_ref, kg_ref, time_ref,
     out_ref,
     x_in, wq, wo, mod, st_in, rows_f, st_src, st_own, st_mate, gran_f,
-    g0, g1, wide, xr, wmod, wodd, weven, perm, wline, pick, colv, gatev, table, gains,
+    g0, g1, wide, xr, wmod, wstack, wodd, weven, perm, wline, pick, colv, gatev, table, gains,
     qsrc, qrecv, merged, stale, stale_f, keys, vals, att, ysrc, dsrc, drecv,
     load_sem, nready, w_send, w_recv,
     ag_send, ag_own, ag_core,
@@ -250,19 +250,27 @@
     first_half = lane < 64
 
     def fold(tick, j):
-        shift_sum = jnp.zeros((QROWS, 128), F32)
-        row_sum = jnp.zeros((QROWS, 128), F32)
         base = times[tick] * 3
-        for k in range(KC):
-            lanes = pl.ds(k * 128, 128)
+
+        def step(k, sums):
+            lanes = pl.ds(pl.multiple_of(k * 128, 128), 128)
             shift = mod[base, :, lanes]
             scale = mod[base + 1, :, lanes]
             w = wq[j, :, lanes].astype(F32)
             scaled = (w * (1.0 + scale)).astype(BF16)
-            wmod[tick, j, :, lanes] = scaled
-            shift_sum += w * shift
-            row_sum += scaled.astype(F32)
-        for n, value in enumerate((shift_sum, row_sum)):
+            wide_scaled = scaled.astype(F32)
+            if tick == 0:
+                wmod[j, :, lanes] = scaled
+            else:
+                padded = jnp.concatenate([wide_scaled, jnp.zeros((8, 128), F32)], axis=0)
+                low = pl.multiple_of((j * 4 + k // 6) * 80, 16)
+                to = pl.ds(pl.multiple_of((k % 6) * 128, 128), 128)
+                wstack[pl.ds(low, 80), to] = padded.astype(BF16)
+            return sums[0] + w * shift, sums[1] + wide_scaled
+
+        zero = jnp.zeros((QROWS, 128), F32)
+        sums = lax.fori_loop(0, KC, step, (zero, zero))
+        for n, value in enumerate(sums):
             total = jnp.sum(value, axis=1, keepdims=True)
             colv[tick, n, j] = jnp.broadcast_to(total, (QROWS, 128))
 
@@ -273,16 +281,30 @@
     gate_sums = []
     for j in range(2):
         mine = (z * 4 + 2 * j + core) * BLK + row
-        sums = [jnp.zeros((BLK, 128), F32), jnp.zeros((BLK, 128), F32)]
-        for k in range(KC):
-            lanes = pl.ds(k * 128, 128)
+
+        def gate_step(k, sums, j=j, mine=mine):
+            lanes = pl.ds(pl.multiple_of(k * 128, 128), 128)
             here = feature + k * 128 == mine
-            pick[j, :, lanes] = jnp.where(here, 1.0, 0.0).astype(BF16)
-            for tick in range(2):
-                sums[tick] += jnp.where(here, mod[times[tick] * 3 + 2, :, lanes], 0.0)
+            pick[pl.ds(j * BLK, BLK), lanes] = jnp.where(here, 1.0, 0.0).astype(BF16)
+            return tuple(
+                v + jnp.where(here, mod[times[tick] * 3 + 2, :, lanes], 0.0)
+                for tick, v in enumerate(sums)
+            )
+
+        zero = jnp.zeros((BLK, 128), F32)
+        sums = lax.fori_loop(0, KC, gate_step, (zero, zero))
         gate_sums.append([jnp.sum(v, axis=1, keepdims=True) for v in sums])
     for tick in range(2):
         gatev[tick] = jnp.where(first_half[:BLK], gate_sums[0][tick], gate_sums[1][tick])
+
+    fold(1, xl)
+    pf = lax.broadcasted_iota(jnp.int32, (CHUNK, 128), 0)
+    po = lax.broadcasted_iota(jnp.int32, (CHUNK, 128), 1)
+    for k in range(CHUNK // 128):
+        to = po + (k % 3) * 128
+        group = jnp.where(to >= 96, 1, 0) + jnp.where(to >= 192, 1, 0) + jnp.where(to >= 288, 1, 0)
+        source = to + 96 * group + 96 * (k // 3)
+        perm[:, pl.ds(k * 128, 128)] = jnp.where(pf == source, 1.0, 0.0).astype(BF16)
 
     @pl.when(owned == 1)
     def _():
@@ -375,7 +397,7 @@
         narrow = piece.astype(BF16)
         xr[pl.ds(0, 64), lanes] = narrow
         xr[pl.ds(64, 64), lanes] = narrow
-    acc_own = dot_nt(wmod[0, xl], xr[...])
+    acc_own = dot_nt(wmod[xl], xr[...])
     mean_c = jnp.sum(total, axis=1, keepdims=True) * (1.0 / D)
     total = jnp.zeros((64, 128), F32)
     for k in range(KC):
@@ -389,8 +411,20 @@
     take(wq.at[1 - xl], w_recv.at[0])
     push(wo.at[xl], wo.at[xl], w_send.at[2], w_recv.at[2], s, x_mate)
     fold(0, 1 - xl)
-    send_qkv(0, 1 - xl, dot_nt(wmod[0, 1 - xl], xr[...]), mean0, var0)
+    send_qkv(0, 1 - xl, dot_nt(wmod[1 - xl], xr[...]), mean0, var0)
     send_stale(1)
+
+    picked = dot_nt(pick[...], xr[...])
+    residual = jnp.where(first_half[:BLK], picked[:BLK], picked[BLK:])
+    fold(1, 1 - xl)
+    moved = dot_nn(wstack[...], perm[...]).astype(BF16)
+    half = CHUNK // 2
+    for j in range(2):
+        for k in range(D // CHUNK):
+            rows = moved[(j * 4 + k) * 80 : (j * 4 + k + 1) * 80]
+            lanes = pl.ds(k * half, half)
+            wline[pl.ds(j * 160, 80), lanes] = rows[:, :half]
+            wline[pl.ds(j * 160 + 80, 80), lanes] = rows[:, half:]
 
     def unpack_stale(tick):
         take(stale.at[tick], st_recv.at[tick])
@@ -511,30 +545,12 @@
     def _():
         send_attended(0)
 
-    picked = [dot_nt(pick[j], xr[...]) for j in range(2)]
-    residual = jnp.where(first_half[:BLK], picked[0], picked[1])
     take(wo.at[1 - xl], w_recv.at[2])
     for j in range(2):
         for pair in range(PAIRS):
             at = pl.ds(j * BLK, BLK), pl.ds(pair * 128, 128)
             weven[at] = wo[j, :, pl.ds(pair * 256, 128)]
             wodd[at] = wo[j, :, pl.ds(pair * 256 + 128, 128)]
-    pf = lax.broadcasted_iota(jnp.int32, (CHUNK, 128), 0)
-    po = lax.broadcasted_iota(jnp.int32, (CHUNK, 128), 1)
-    for k in range(CHUNK // 128):
-        to = po + (k % 3) * 128
-        group = jnp.where(to >= 96, 1, 0) + jnp.where(to >= 192, 1, 0) + jnp.where(to >= 288, 1, 0)
-        source = to + 96 * group + 96 * (k // 3)
-        perm[:, pl.ds(k * 128, 128)] = jnp.where(pf == source, 1.0, 0.0).astype(BF16)
-    half = CHUNK // 2
-    for j in range(2):
-        fold(1, j)
-        for k in range(D // CHUNK):
-            moved = dot_nn(wmod[1, j, :, pl.ds(k * CHUNK, CHUNK)], perm[...])
-            moved = jnp.concatenate([moved, jnp.zeros((8, CHUNK), F32)], axis=0).astype(BF16)
-            lanes = pl.ds(k * half, half)
-            wline[pl.ds(j * 160, 80), lanes] = moved[:, :half]
-            wline[pl.ds(j * 160 + 80, 80), lanes] = moved[:, half:]
 
     gather_attended(0)
     ysrc[...] = project(0, residual)
@@ -618,12 +634,13 @@
             pltpu.VMEM((LINE * BLK, 128), BF16),
             pltpu.VMEM((LINE * BLK, 128), F32),
             pltpu.VMEM((128, D), BF16),
-            pltpu.VMEM((2, 2, QROWS, D), BF16),
+            pltpu.VMEM((2, QROWS, D), BF16),
+            pltpu.VMEM((640, CHUNK), BF16),
             pltpu.VMEM((2 * BLK, D // 4), BF16),
             pltpu.VMEM((2 * BLK, D // 4), BF16),
             pltpu.VMEM((CHUNK, CHUNK), BF16),
             pltpu.VMEM((320, D // 2), BF16),
-            pltpu.VMEM((2, BLK, D), BF16),
+            pltpu.VMEM((2 * BLK, D), BF16),
             pltpu.VMEM((2, 2, 2, QROWS, 128), F32),
             pltpu.VMEM((2, BLK, 128), F32),
             pltpu.VMEM((2, 64, 128), F32),

time: 87.8 us -> 87.6 us (level)
  no operation moved by 1% of the time
where the time goes in v6:
time: 87.6 us; the launch traced here: 87.4 us
  Pallas kernels  85.8 us (98%)
    pallas_call x1, Pallas kernels, per_device(): pl.pallas_call(kernel, out_shape=jax.ShapeDtypeStruct((LINE, 2, 128), F32...  85.8 us

profile of v6, /device:TPU:1, one launch (start us, length us, event | category | flops | bytes accessed | tf_op | source)
XLA Modules:
  0.0 87.4 jit_solution(6962103026706152152)
XLA Ops:
  0.0 85.8 %block_cycle.1 = f32[32,2,128]{2,1,0:T(2,128)} custom-call(bf16[2,3072]{1,0:T(2,128)(2,1)} %bitcast.16, bf16[72,3072]{1,0:T(8,128)(2,1)} %bitcast.13, bf16[48,1536]{1,0:T(8,128)(2,1)} %bitcast.14, f32[84,1,3072]{2,1,0:T(1,128)} %bitcast.12, bf16[8,2,3072]{2,1,0:T(2,128)(2,1)} %bitcast.15, s32[1,64]{1,0:T(1,128)} %bitcast.17, f32[1,128]{1,0:T(1,128)} %qg_ref.1, ...), custom_call_target="tpu_custom_call" | custom-call | tf_op jit(solution)/shard_map/block_cycle/pallas_call | solution.py:617
  85.8 0.8 convert.4
  86.5 0.1 reshape.22
  86.7 0.7 convert_element_type.16
  (2 shorter events, 0.1 us)

commit v7 on v6

--- a/solution.py
+++ b/solution.py
@@ -412,7 +412,6 @@
     push(wo.at[xl], wo.at[xl], w_send.at[2], w_recv.at[2], s, x_mate)
     fold(0, 1 - xl)
     send_qkv(0, 1 - xl, dot_nt(wmod[1 - xl], xr[...]), mean0, var0)
-    send_stale(1)
 
     picked = dot_nt(pick[...], xr[...])
     residual = jnp.where(first_half[:BLK], picked[:BLK], picked[BLK:])
@@ -425,6 +424,7 @@
             lanes = pl.ds(k * half, half)
             wline[pl.ds(j * 160, 80), lanes] = rows[:, :half]
             wline[pl.ds(j * 160 + 80, 80), lanes] = rows[:, half:]
+    send_stale(1)
 
     def unpack_stale(tick):
         take(stale.at[tick], st_recv.at[tick])

time: 87.6 us -> 86.9 us (level)
  Pallas kernels: 85.8 us -> 84.6 us
    pallas_call x1, Pallas kernels: 85.8 us -> 84.6 us  [per_device(): pl.pallas_call(kernel, out_shape=jax.ShapeDtypeStruct((LINE, 2, 128), F32...]
where the time goes in v7:
time: 86.9 us; the launch traced here: 86.3 us
  Pallas kernels  84.6 us (97%)
    pallas_call x1, Pallas kernels, per_device(): pl.pallas_call(kernel, out_shape=jax.ShapeDtypeStruct((LINE, 2, 128), F32...  84.6 us

profile of v7, /device:TPU:1, one launch (start us, length us, event | category | flops | bytes accessed | tf_op | source)
XLA Modules:
  0.0 86.3 jit_solution(16728891798595914199)
XLA Ops:
  0.0 84.6 %block_cycle.1 = f32[32,2,128]{2,1,0:T(2,128)} custom-call(bf16[2,3072]{1,0:T(2,128)(2,1)} %bitcast.16, bf16[72,3072]{1,0:T(8,128)(2,1)} %bitcast.13, bf16[48,1536]{1,0:T(8,128)(2,1)} %bitcast.14, f32[84,1,3072]{2,1,0:T(1,128)} %bitcast.12, bf16[8,2,3072]{2,1,0:T(2,128)(2,1)} %bitcast.15, s32[1,64]{1,0:T(1,128)} %bitcast.17, f32[1,128]{1,0:T(1,128)} %qg_ref.1, ...), custom_call_target="tpu_custom_call" | custom-call | tf_op jit(solution)/shard_map/block_cycle/pallas_call | solution.py:617
  84.6 0.8 convert.4
  85.4 0.1 reshape.22
  85.6 0.7 convert_element_type.16
  (2 shorter events, 0.1 us)
